TPU v7x, 256 devices: a whole 4x4x8 slice. The times are simulated.
256 devices in a mesh: level: 16 (over x_lo, y, core), slab: 16 (over x_hi, z).
Axes of the slice: x: 4 (x_hi: 2, x_lo: 2; x = x_hi * 2 + x_lo), y: 4, z: 8, core: 2. Of those that a mesh axis runs over, the one named last changes fastest.
Arguments:
- right_side: float32 [64, 256, 512], P('slab', 'level'), may hold values from -6 to 6
- scale_field: float32 [64, 256, 512], P('slab', 'level'), may hold values from 0.7 to 1.4
- mass_field: float32 [64, 256, 512], P('slab', 'level'), may hold values from 0.05 to 0.5
- degrees: int32 [3], replicated, may hold values from 2 to 6, as said below
- lower_bound: float32 [3], replicated, may hold values from 0.05 to 0.3
- upper_bound: float32 [3], replicated, may hold values from 2 to 2.6
Outputs:
- solution: float32 [64, 256, 512], P('slab', 'level')
- final_res: float32 [64, 256, 512], P('slab', 'level')
Inputs may be any that keep to these rules, and one draw needn't show every extreme that they name: `degrees`: degree of each grid; in every draw at least one grid has degree exactly 6.
All inputs are finite; a program needn't handle non-finite values.
Results may differ from a plain program's by a relative error of at most 0.0001.
Values sent between devices are 32-bit elements; how exact they have to be, the bound alone decides.
A program may use at most 128 MiB of HBM per device.

v0:
```python
import jax
import jax.numpy as jnp
from jax import lax
from jax.sharding import PartitionSpec as P

CYCLES = 3
MAXDEG = 6


def extended(shard, sides, width):
    for axis, dim in sides:
        peers, length = (lax.axis_size(axis), shard.shape[dim])
        up = [(i, (i + 1) % peers) for i in range(peers - 1)]
        down = [(j, i) for i, j in up]
        last = lax.slice_in_dim(shard, length - width, length, axis=dim)
        first = lax.slice_in_dim(shard, 0, width, axis=dim)
        before = lax.ppermute(last, axis, up)
        after = lax.ppermute(first, axis, down)
        shard = jnp.concatenate([before, shard, after], axis=dim)
    return shard


def box_sum(padded):
    summed = padded[:-2] + padded[1:-1] + padded[2:]
    summed = summed[:, :-2] + summed[:, 1:-1] + summed[:, 2:]
    return summed[:, :, :-2] + summed[:, :, 1:-1] + summed[:, :, 2:]


def finish(padded_zx, weighted, field, coeff, mass_term):
    padded = jnp.pad(padded_zx, ((0, 0), (0, 0), (1, 1)))
    return coeff * (27.0 / 26.0 * weighted - box_sum(padded) / 26.0) + mass_term * field


def fine_apply(field, coeff, mass_term):
    weighted = coeff * field
    padded = extended(weighted, (("level", 1), ("slab", 0)), 1)
    return finish(padded, weighted, field, coeff, mass_term)


def mid_apply(field, coeff, mass_term):
    weighted = coeff * field
    padded = extended(weighted, (("level", 1), ("slab", 0)), 1)
    return finish(padded, weighted, field, coeff, mass_term)


def coarse_apply(field, coeff, mass_term):
    weighted = coeff * field
    padded = extended(weighted, (("level", 1), ("slab", 0)), 1)
    return finish(padded, weighted, field, coeff, mass_term)


def average_cells(field):
    size_z, size_x, size_y = field.shape
    blocks = field.reshape(size_z // 2, 2, size_x // 2, 2, size_y // 2, 2)
    return jnp.mean(blocks, axis=(1, 3, 5))


def prolong(field):
    size_z, size_x, size_y = field.shape
    spread_out = jnp.broadcast_to(
        field[:, None, :, None, :, None], (size_z, 2, size_x, 2, size_y, 2)
    )
    return spread_out.reshape(2 * size_z, 2 * size_x, 2 * size_y)


def prepare(source, coeff, mass_term, bound_low, bound_high):
    inverse = 1.0 / (coeff * coeff + mass_term)
    centre = (bound_high + bound_low) * 0.5
    radius = (bound_high - bound_low) * 0.5
    spread_ratio = centre / radius
    direction = inverse * source / centre
    rho_now = 1.0 / spread_ratio
    return ((inverse, spread_ratio, radius), (direction, direction, rho_now))


def advance(operator, source, coeff, mass_term, constants, state_now):
    inverse, spread_ratio, radius = constants
    approx, old_dir, rho_old = state_now
    defect = source - operator(approx, coeff, mass_term)
    rho_new = 1.0 / (2.0 * spread_ratio - rho_old)
    new_dir = rho_new * rho_old * old_dir + 2.0 * rho_new / radius * inverse * defect
    return (approx + new_dir, new_dir, rho_new)


def keep_active(active, stepped, state_now):
    return tuple(
        (jnp.where(active, new_val, old_val) for new_val, old_val in zip(stepped, state_now))
    )


def smooth(operator, source, coeff, mass_term, degree, bound_low, bound_high):
    constants, start_state = prepare(source, coeff, mass_term, bound_low, bound_high)

    def sweep_turn(step_no, state_now):
        stepped = advance(operator, source, coeff, mass_term, constants, state_now)
        return keep_active(step_no < degree, stepped, state_now)

    result = lax.fori_loop(1, MAXDEG, sweep_turn, start_state)
    return result[0]


def shards(right_side, scale_field, mass_field, degrees, lower_bound, upper_bound):
    scale_mid = average_cells(scale_field)
    mass_mid = average_cells(mass_field)
    scale_low = average_cells(scale_mid)
    mass_low = average_cells(mass_mid)
    solution = jnp.zeros_like(right_side)
    for cycle_no in range(CYCLES):
        if cycle_no == 0:
            resid = right_side
        else:
            resid = right_side - fine_apply(solution, scale_field, mass_field)
        resid_mid = 4.0 * average_cells(resid)
        resid_low = 4.0 * average_cells(resid_mid)
        fine_task = (
            fine_apply,
            resid,
            scale_field,
            mass_field,
            degrees[0],
            lower_bound[0],
            upper_bound[0],
        )
        mid_task = (
            mid_apply,
            resid_mid,
            scale_mid,
            mass_mid,
            degrees[1],
            lower_bound[1],
            upper_bound[1],
        )
        low_task = (
            coarse_apply,
            resid_low,
            scale_low,
            mass_low,
            degrees[2],
            lower_bound[2],
            upper_bound[2],
        )
        fine_corr = smooth(*fine_task)
        mid_corr = smooth(*mid_task)
        low_out = smooth(*low_task)
        solution = solution + 0.5 * (fine_corr + prolong(mid_corr + prolong(low_out)))
    final_res = right_side - fine_apply(solution, scale_field, mass_field)
    return (solution, final_res)


def solution(mesh):
    return jax.shard_map(
        shards,
        mesh=mesh,
        in_specs=(
            P("slab", "level", None),
            P("slab", "level", None),
            P("slab", "level", None),
            P(),
            P(),
            P(),
        ),
        out_specs=(P("slab", "level", None), P("slab", "level", None)),
        check_vma=False,
    )
```

profile of v0, /device:TPU:6, one launch (start us, length us, event | category | flops | bytes accessed | tf_op | source)
XLA Modules:
  0.0 1117.2 jit_solution(8839591993241308204)
XLA Ops:
  4.8 10.6 reshape.229
  15.4 9.7 reshape.228
  25.1 9.8 reshape.227
  55.0 110.0 %while.173 = (s32[]{:T(128)}, f32[1,4,128]{2,1,0:T(4,128)S(1)}, f32[1,4,128]{2,1,0:T(4,128)S(1)}, f32[]{:T(128)}, s32[]{:T(128)}, /*index=5*/f32[]{:T(128)}, f32...) while((s32[]{:T(128)}, f32[1,4,128]{2,1,0:T(4,128)S(1)}, ...), condition=%wide.region_14.15_spmd, body=%wide.region_13.14_spmd.sunk | while | flops 40929 | bytes 113489 | solution.py:98
  61.6 5.0 collective-permute-done.9
  66.6 8.3 collective-permute-start.10
  77.6 6.5 collective-permute-done.11
  165.5 102.2 %while.172 = (s32[]{:T(128)}, f32[2,8,256]{2,1,0:T(8,128)S(1)}, f32[2,8,256]{2,1,0:T(8,128)S(1)}, f32[]{:T(128)}, s32[]{:T(128)}, /*index=5*/f32[]{:T(128)}, f32...) while((s32[]{:T(128)}, f32[2,8,256]{2,1,0:T(8,128)S(1)}, ...), condition=%wide.region_6.7_spmd, body=%wide.region_5.0_spmd.sunk | while | flops 222297 | bytes 714561 | solution.py:98
  271.5 6.9 reshape.230
  278.5 105.7 %while.171 = (s32[]{:T(128)}, f32[4,16,512]{2,1,0:T(8,128)S(1)}, f32[4,16,512]{2,1,0:T(8,128)S(1)}, f32[]{:T(128)}, s32[]{:T(128)}, /*index=5*/f32[]{:T(128)}, f...) while((s32[]{:T(128)}, f32[4,16,512]{2,1,0:T(8,128)S(1)}, ...), condition=%wide.region_1.0_spmd, body=%wide.region_0.0_spmd.sunk | while | flops 1399881 | bytes 4535777 | solution.py:98
  336.5 4.9 collective-permute-done.3
  399.3 5.5 collective-permute-done.38
  405.2 9.8 reshape.231
  419.7 101.0 %while.176 = (s32[]{:T(128)}, f32[1,4,128]{2,1,0:T(4,128)S(1)}, f32[1,4,128]{2,1,0:T(4,128)S(1)}, f32[]{:T(128)}, s32[]{:T(128)}, /*index=5*/f32[]{:T(128)}, f32...) while((s32[]{:T(128)}, f32[1,4,128]{2,1,0:T(4,128)S(1)}, ...), condition=%wide.region_23.24_spmd, body=%wide.region_22.23_spmd.sunk | while | flops 40929 | bytes 113489 | solution.py:98
  521.1 102.2 %while.175 = (s32[]{:T(128)}, f32[2,8,256]{2,1,0:T(8,128)S(1)}, f32[2,8,256]{2,1,0:T(8,128)S(1)}, f32[]{:T(128)}, s32[]{:T(128)}, /*index=5*/f32[]{:T(128)}, f32...) while((s32[]{:T(128)}, f32[2,8,256]{2,1,0:T(8,128)S(1)}, ...), condition=%wide.region_19.20_spmd, body=%wide.region_18.19_spmd.sunk | while | flops 222297 | bytes 714561 | solution.py:98
  627.2 6.9 reshape.232
  634.1 105.7 %while.174 = (s32[]{:T(128)}, f32[4,16,512]{2,1,0:T(8,128)S(1)}, f32[4,16,512]{2,1,0:T(8,128)S(1)}, f32[]{:T(128)}, s32[]{:T(128)}, /*index=5*/f32[]{:T(128)}, f...) while((s32[]{:T(128)}, f32[4,16,512]{2,1,0:T(8,128)S(1)}, ...), condition=%wide.region_16.17_spmd, body=%wide.region_15.16_spmd.sunk | while | flops 1399881 | bytes 4535777 | solution.py:98
  755.0 5.4 collective-permute-done.42
  760.9 9.8 reshape.233
  775.4 101.0 %while.179 = (s32[]{:T(128)}, f32[1,4,128]{2,1,0:T(4,128)S(1)}, f32[1,4,128]{2,1,0:T(4,128)S(1)}, f32[]{:T(128)}, s32[]{:T(128)}, /*index=5*/f32[]{:T(128)}, f32...) while((s32[]{:T(128)}, f32[1,4,128]{2,1,0:T(4,128)S(1)}, ...), condition=%wide.region_32.33_spmd, body=%wide.region_31.32_spmd.sunk | while | flops 40929 | bytes 113489 | solution.py:98
  876.7 102.2 %while.178 = (s32[]{:T(128)}, f32[2,8,256]{2,1,0:T(8,128)S(1)}, f32[2,8,256]{2,1,0:T(8,128)S(1)}, f32[]{:T(128)}, s32[]{:T(128)}, /*index=5*/f32[]{:T(128)}, f32...) while((s32[]{:T(128)}, f32[2,8,256]{2,1,0:T(8,128)S(1)}, ...), condition=%wide.region_28.29_spmd, body=%wide.region_27.28_spmd.sunk | while | flops 222297 | bytes 714561 | solution.py:98
  982.8 6.9 reshape.234
  989.8 105.7 %while.177 = (s32[]{:T(128)}, f32[4,16,512]{2,1,0:T(8,128)S(1)}, f32[4,16,512]{2,1,0:T(8,128)S(1)}, f32[]{:T(128)}, s32[]{:T(128)}, /*index=5*/f32[]{:T(128)}, f...) while((s32[]{:T(128)}, f32[4,16,512]{2,1,0:T(8,128)S(1)}, ...), condition=%wide.region_25.26_spmd, body=%wide.region_24.25_spmd.sunk | while | flops 1399881 | bytes 4535777 | solution.py:98
  1110.5 5.5 collective-permute-done.46
  (833 shorter events, 957.6 us)
Async XLA Ops:
  66.6 11.0 collective-permute-start.10
  176.4 9.2 collective-permute-start.7
  196.8 9.2 collective-permute-start.7
  237.7 9.2 collective-permute-start.7
  258.1 9.2 collective-permute-start.7
  289.5 9.6 collective-permute-start.3
  310.6 9.6 collective-permute-start.3
  331.8 9.6 collective-permute-start.3
  352.9 9.6 collective-permute-start.3
  374.0 9.6 collective-permute-start.3
  395.2 9.6 collective-permute-start.38
  532.0 9.2 collective-permute-start.19
  645.1 9.6 collective-permute-start.15
  666.3 9.6 collective-permute-start.15
  687.4 9.6 collective-permute-start.15
  708.5 9.6 collective-permute-start.15
  729.7 9.6 collective-permute-start.15
  750.8 9.6 collective-permute-start.42
  1000.8 9.6 collective-permute-start.27
  1021.9 9.6 collective-permute-start.27
  1043.0 9.6 collective-permute-start.27
  1064.2 9.6 collective-permute-start.27
  1085.3 9.6 collective-permute-start.27
  1106.5 9.6 collective-permute-start.46
  (173 other events, 1173.4 us)
where the time goes:
time: 1120 us
  starting transfers between devices  495 us (44%)
  waiting for transfers between devices  448 us (40%)
  local copies, waits for them, and re-layouts  88.1 us (8%)
  loops' own time  38.7 us (3%)
  other arithmetic  37.7 us (3%)
    ppermute x96, waiting for transfers between devices, extended(): before = lax.ppermute(last, axis, up)  448 us
    ppermute x96, starting transfers between devices, extended(): before = lax.ppermute(last, axis, up)  302 us
    ppermute x96, starting transfers between devices, extended(): after = lax.ppermute(first, axis, down)  193 us
    reshape x5, local copies, waits for them, and re-layouts, average_cells(): blocks = field.reshape(size_z // 2, 2, size_x // 2, 2, size_y // 2, 2)  49.5 us
    another operation x9, loops' own time, smooth(): result = lax.fori_loop(1, MAXDEG, sweep_turn, start_state)  38.7 us
  transfers between devices with their start and end apart: 192, of which 97 were waited for; matrix products, arithmetic and copies ran while one was open for 0% of the time, Pallas kernels for 0%

commit v1 on v0

v1 whole, which is shorter than its diff:
```python
import jax
import jax.numpy as jnp
from jax import lax
from jax.experimental import pallas as pl
from jax.experimental.pallas import tpu as pltpu
from jax.sharding import PartitionSpec as P

CYCLES = 3
MAXDEG = 6
DEPTH = 6
PEERS = 16
LANES = 128
MESH = pl.DeviceIdType.MESH
f32 = jnp.float32


def split_matrices():
    row = lax.broadcasted_iota(jnp.int32, (LANES, LANES), 0)
    col = lax.broadcasted_iota(jnp.int32, (LANES, LANES), 1)
    spread = [jnp.where(row == half * 64 + col // 2, 1.0, 0.0).astype(f32) for half in (0, 1)]
    gather = [jnp.where(col == half * 64 + row // 2, 1.0, 0.0).astype(f32) for half in (0, 1)]
    return spread, gather


def dot(a, b):
    return jnp.dot(a, b, preferred_element_type=f32, precision=lax.Precision.HIGHEST)


def kernel(
    rhs, scale, mass, degrees, lower, upper, sol_out, res_out,
    gf, kf, cf, wf, df, sf, pf, jf, tmp_c, tmp_q, tmp_r,
    gm, km, im, wm, dm, em, pm, jm, mid_c, mid_q, mid_r,
    lb, gl, kl, il, wl, dl, el, jl,
    coef, send_sem, recv_sem,
):
    s = lax.axis_index("slab")
    l = lax.axis_index("level")
    count = [0]
    pending = []

    for ref in (gf.at[0], gf.at[1], gf.at[2], kf, cf, wf.at[0], wf.at[1],
                gm.at[0], gm.at[1], gm.at[2], km, im, wm.at[0], wm.at[1],
                gl, kl, il, wl.at[0], wl.at[1], el, em):
        def clear(z, carry, ref=ref):
            ref[z] = jnp.zeros(ref.shape[1:], f32)
            return carry
        lax.fori_loop(0, ref.shape[0], clear, 0)
    for kind in range(5):
        def clear_blocks(z, carry, kind=kind):
            lb[kind, z] = jnp.zeros((5, 4, LANES), f32)
            return carry
        lax.fori_loop(0, 13, clear_blocks, 0)

    barrier = pltpu.get_barrier_semaphore()
    for step in range(1, 7):
        for sign in (1, -1):
            @pl.when((s + sign * step >= 0) & (s + sign * step < PEERS))
            def _(step=step, sign=sign):
                pl.semaphore_signal(barrier, inc=1, device_id={"slab": s + sign * step, "level": l}, device_id_type=MESH)
    for step in range(1, 3):
        for sign in (1, -1):
            @pl.when((l + sign * step >= 0) & (l + sign * step < PEERS))
            def _(step=step, sign=sign):
                pl.semaphore_signal(barrier, inc=1, device_id={"slab": s, "level": l + sign * step}, device_id_type=MESH)

    class Message:
        def __init__(self, src, dst, ds=0, dl=0):
            self.at = count[0]
            count[0] += 1
            self.src, self.dst, self.ds, self.dl = src, dst, ds, dl
            pending.append(self)

        def copy(self):
            return pltpu.make_async_remote_copy(
                src_ref=self.src, dst_ref=self.dst,
                send_sem=send_sem.at[self.at], recv_sem=recv_sem.at[self.at],
                device_id={"slab": s + self.ds, "level": l + self.dl}, device_id_type=MESH,
            )

        def valid(self, sign):
            at, step = (s, self.ds) if self.ds else (l, self.dl)
            return (at + sign * step >= 0) & (at + sign * step < PEERS)

        def start(self):
            @pl.when(self.valid(1))
            def _():
                self.copy().start()

        def arrived(self):
            @pl.when(self.valid(-1))
            def _():
                self.copy().wait_recv()

        def sent(self):
            @pl.when(self.valid(1))
            def _():
                self.copy().wait_send()

    def start(messages):
        for m in messages:
            m.start()
        return messages

    def arrived(messages):
        for m in messages:
            m.arrived()

    def z_messages(view, own, depth, hop):
        layers = max(0, min(own, depth - own * (hop - 1)))
        if layers == 0:
            return []
        gap = own * (hop - 1)
        top, bottom = 6 + own, 6
        return [
            Message(view(top - layers, layers), view(6 - gap - layers, layers), ds=hop),
            Message(view(bottom, layers), view(top + gap, layers), ds=-hop),
        ]

    def x_messages(buf, first, planes, width):
        cut = lambda row: buf.at[pl.ds(first, planes), :, pl.ds(row, 8), :]
        return [
            Message(cut(16 + width - 8), cut(8), dl=1),
            Message(cut(16), cut(16 + width), dl=-1),
        ]

    def low_x_messages(kind, depth):
        cut = lambda block: lb.at[kind, pl.ds(6 - depth, 1 + 2 * depth), block]
        return [Message(cut(2), cut(2 - step), dl=step) for step in (1, -1, 2, -2)]

    fine_view = lambda buf: (lambda first, layers: buf.at[pl.ds(first, layers), :, pl.ds(16, 16), :])
    mid_view = lambda buf: (lambda first, layers: buf.at[pl.ds(first, layers), :, pl.ds(16, 8), :])
    low_view = lambda kind: (lambda first, layers: lb.at[kind, pl.ds(first, layers), 2])

    for grid in range(3):
        low_b = jnp.full((8, LANES), lower[grid], f32)
        high_b = jnp.full((8, LANES), upper[grid], f32)
        degree = jnp.full((8, LANES), degrees[grid], jnp.int32)
        centre = (high_b + low_b) * 0.5
        radius = (high_b - low_b) * 0.5
        ratio = centre / radius
        rho = 1.0 / ratio
        coef[grid, 0, 0] = 1.0 / centre
        for j in range(1, MAXDEG):
            rho_new = 1.0 / (2.0 * ratio - rho)
            active = j < degree
            coef[grid, j, 0] = jnp.where(active, rho_new * rho, 0.0)
            coef[grid, j, 1] = jnp.where(active, 2.0 * rho_new / radius, 0.0)
            rho = rho_new

    spread, gather = split_matrices()
    lane = lax.broadcasted_iota(jnp.int32, (1, LANES), 1)

    def tile_rows(v, rows):
        return jnp.concatenate([v] * (rows // 8), axis=0) if rows > 8 else v

    def x_sum(ref, z, tiles, r0, rows):
        return tuple(
            ref[z, t, pl.ds(r0 - 1, rows), :] + ref[z, t, pl.ds(r0, rows), :] + ref[z, t, pl.ds(r0 + 1, rows), :]
            for t in range(tiles)
        )

    def y_sum(vals):
        right = [pltpu.roll(v, 1, 1) for v in vals]
        left = [pltpu.roll(v, LANES - 1, 1) for v in vals]
        out = []
        for t, v in enumerate(vals):
            before = right[t - 1] if t > 0 else 0.0
            after = left[t + 1] if t + 1 < len(vals) else 0.0
            out.append(v + jnp.where(lane == 0, before, right[t]) + jnp.where(lane == LANES - 1, after, left[t]))
        return out

    def sweep(src, lo, hi, tiles, r0, rows, use):
        first = (x_sum(src, lo - 1, tiles, r0, rows), x_sum(src, lo, tiles, r0, rows))

        def plane(z, carry):
            below, here = carry
            above = x_sum(src, z + 1, tiles, r0, rows)
            box = y_sum([a + b + c for a, b, c in zip(below, here, above)])
            use(z, box)
            return here, above

        unroll = 2 if (hi - lo) % 2 == 0 else 1
        lax.fori_loop(lo, hi, plane, first, unroll=unroll)

    def smooth(grid, g, k, w, d, own, tiles, chunks):
        planes = own + 2 * DEPTH
        for j in range(1, MAXDEG):
            new = w.at[(j - 1) % 2]
            old = g if j == 1 else w.at[j % 2]
            for r0, rows in chunks:
                a = tile_rows(coef[grid, j, 0], rows)
                b = tile_rows(coef[grid, j, 1], rows)
                first = tile_rows(coef[grid, 0, 0], rows)

                def use(z, box, j=j, r0=r0, rows=rows, a=a, b=b, first=first, new=new, old=old):
                    cut = pl.ds(r0, rows)
                    for t in range(tiles):
                        source = g[z, t, cut, :]
                        if j == 1:
                            here = source * first
                            total = box[t] * first
                            direction = here
                        else:
                            here = old[z, t, cut, :]
                            total = box[t]
                            direction = d[z, t, cut, :]
                        defect = (source - here) + k[z, t, cut, :] * (total - here)
                        direction = a * direction + b * defect
                        d[z, t, cut, :] = direction
                        new[z, t, cut, :] = here + direction

                sweep(old, j, planes - j, tiles, r0, rows, use)

    def restrict(src, planes, tiles, rows):
        result = []
        for z in range(planes // 2):
            sums = []
            for t in range(tiles):
                total = None
                for dz in (0, 1):
                    for dx in (0, 1):
                        part = src[2 * z + dz, t, pl.ds(dx, rows, stride=2), :]
                        total = part if total is None else total + part
                sums.append(total * 0.125)
            result.append([
                dot(sums[2 * o], gather[0]) + dot(sums[2 * o + 1], gather[1]) for o in range(tiles // 2)
            ])
        return result

    for z in range(4):
        for t in range(4):
            cut = pl.ds(t * LANES, LANES)
            c = scale[z, :, cut]
            q = mass[z, :, cut]
            diag = c * c + q
            inverse = 1.0 / diag
            tmp_c[z, t] = c
            tmp_q[z, t] = q
            jf[z, t] = diag / c
            b = rhs[z, :, cut]
            tmp_r[z, t] = b
            kf[6 + z, t, pl.ds(16, 16), :] = c * c * inverse * (1.0 / 26.0)
            cf[6 + z, t, pl.ds(16, 16), :] = c
            gf[0, 6 + z, t, pl.ds(16, 16), :] = c * inverse * b

    greet = jnp.minimum(s, 6) + jnp.minimum(PEERS - 1 - s, 6) + jnp.minimum(l, 2) + jnp.minimum(PEERS - 1 - l, 2)
    pl.semaphore_wait(barrier, greet)

    for cycle in range(CYCLES):
        first = cycle == 0
        fine = [(gf.at[cycle], DEPTH)] + ([(kf, DEPTH - 1)] if first else [])
        near, far, side = [], [], []
        for buf, depth in fine:
            near += z_messages(fine_view(buf), 4, depth, 1)
            side += x_messages(buf, 6, 4, 16)
            far += z_messages(fine_view(buf), 4, depth, 2)
        if first:
            near += z_messages(fine_view(cf), 4, 1, 1)
        start(near)
        start(side)

        if first:
            cs, qs = restrict(tmp_c, 4, 4, 8), restrict(tmp_q, 4, 4, 8)
            for z in range(2):
                for t in range(2):
                    c, q = cs[z][t], qs[z][t]
                    diag = c * c + q
                    mid_c[z, t] = c
                    mid_q[z, t] = q
                    jm[z, t] = c / diag
                    km[6 + z, t, pl.ds(16, 8), :] = c * c / diag * (1.0 / 26.0)
                    im[6 + z, t, pl.ds(16, 8), :] = 1.0 / c
            c, q = restrict(mid_c, 2, 2, 4)[0][0], restrict(mid_q, 2, 2, 4)[0][0]
            diag = c * c + q
            jl[...] = c / diag
            lb[3, 6, 2] = c * c / diag * (1.0 / 26.0)
            lb[4, 6, 2] = 1.0 / c
        rs = restrict(tmp_r, 4, 4, 8)
        for z in range(2):
            for t in range(2):
                r = 4.0 * rs[z][t]
                mid_r[z, t] = r
                gm[cycle, 6 + z, t, pl.ds(16, 8), :] = r * jm[z, t]
        lb[cycle, 6, 2] = 4.0 * restrict(mid_r, 2, 2, 4)[0][0] * jl[...]

        kinds = [(cycle, DEPTH)] + ([(3, DEPTH - 1), (4, 1)] if first else [])
        low_z = []
        for kind, depth in kinds:
            for hop in range(1, 7):
                low_z += z_messages(low_view(kind), 1, depth, hop)
        start(low_z)
        mids = [(gm.at[cycle], DEPTH)] + ([(km, DEPTH - 1), (im, 1)] if first else [])
        mid_z = []
        for buf, depth in mids:
            for hop in range(1, 4):
                mid_z += z_messages(mid_view(buf), 2, depth, hop)
        start(mid_z)
        start(far)

        arrived(near)
        for buf, depth in fine:
            side += start(x_messages(buf, 2, 4, 16) + x_messages(buf, 10, 4, 16))
        if first:
            side += start(x_messages(cf, 5, 6, 16))
        arrived(low_z)
        low_x = []
        for kind, depth in kinds:
            low_x += start(low_x_messages(kind, depth))
        arrived(mid_z)
        mid_x = []
        for buf, depth in mids:
            mid_x += start(x_messages(buf, 6 - depth, 2 + 2 * depth, 8))
        arrived(far)
        for buf, depth in fine:
            side += start(x_messages(buf, 6 - depth, depth - 4, 16) + x_messages(buf, 14, depth - 4, 16))

        arrived(low_x)
        for kind, depth in kinds:
            dst = {3: kl, 4: il}.get(kind, gl)
            for block in range(5):
                dst[:, 0, pl.ds(8 + 4 * block, 4), :] = lb[kind, :, block]
        smooth(2, gl, kl, wl, dl, 1, 1, [(8, 24)])
        for z in range(5, 8):
            el[z - 5, 0, pl.ds(8, 24), :] = wl[0, z, 0, pl.ds(8, 24), :] * il[z, 0, pl.ds(8, 24), :]
        for z in range(3):
            coarse = el[z, 0, pl.ds(12, 16), :]
            for t in range(2):
                wide = dot(coarse, spread[t])
                for dx in (0, 1):
                    pm[z, t, pl.ds(8 + dx, 16, stride=2), :] = wide

        arrived(mid_x)
        smooth(1, gm.at[cycle], km, wm, dm, 2, 2, [(8, 24)])
        for z in range(5, 9):
            for t in range(2):
                cut = pl.ds(8, 24)
                em[z - 5, t, cut, :] = wm[0, z, t, cut, :] * im[z, t, cut, :] + pm[(z - 6) // 2 + 1, t, cut, :]
        for z in range(4):
            for t in range(4):
                wide = dot(em[z, t // 2, pl.ds(12, 16), :], spread[t % 2])
                for dx in (0, 1):
                    pf[z, t, pl.ds(8 + dx, 16, stride=2), :] = wide

        arrived(side)
        smooth(0, gf.at[cycle], kf, wf, df, 4, 4, [(8, 16), (24, 16)])
        for z in range(5, 11):
            for t in range(4):
                cut = pl.ds(8, 32)
                step = 0.5 * (wf[0, z, t, cut, :] + cf[z, t, cut, :] * pf[(z - 6) // 2 + 1, t, cut, :])
                sf[z, t, cut, :] = step if first else sf[z, t, cut, :] + step

        def residual(z, box, last=cycle == CYCLES - 1, cycle=cycle):
            cut = pl.ds(16, 16)
            for t in range(4):
                here = sf[z, t, cut, :]
                scaled = gf[0, z, t, cut, :] - here + kf[z, t, cut, :] * (box[t] - here)
                plain = scaled * jf[z - 6, t]
                if last:
                    out = pl.ds(t * LANES, LANES)
                    sol_out[z - 6, :, out] = here / cf[z, t, cut, :]
                    res_out[z - 6, :, out] = plain
                else:
                    gf[cycle + 1, z, t, cut, :] = scaled
                    tmp_r[z - 6, t] = plain

        sweep(sf, 6, 10, 4, 16, 16, residual)

    for m in pending:
        m.sent()


MESSAGES = 192


def shards(right_side, scale_field, mass_field, degrees, lower_bound, upper_bound):
    vmem = lambda *dims: pltpu.VMEM(dims, f32)
    fine, mid, low = (16, 4, 48, LANES), (14, 2, 40, LANES), (13, 1, 40, LANES)
    block = jax.ShapeDtypeStruct(right_side.shape, f32)
    whole = pl.BlockSpec(memory_space=pltpu.VMEM)
    scalar = pl.BlockSpec(memory_space=pltpu.SMEM)
    return pl.pallas_call(
        kernel,
        out_shape=(block, block),
        in_specs=[whole] * 3 + [scalar] * 3,
        out_specs=(whole, whole),
        scratch_shapes=[
            vmem(3, *fine), vmem(*fine), vmem(*fine), vmem(2, *fine), vmem(*fine), vmem(*fine),
            vmem(4, 4, 48, LANES), vmem(4, 4, 16, LANES), vmem(4, 4, 16, LANES), vmem(4, 4, 16, LANES), vmem(4, 4, 16, LANES),
            vmem(3, *mid), vmem(*mid), vmem(*mid), vmem(2, *mid), vmem(*mid), vmem(4, 2, 40, LANES),
            vmem(3, 2, 40, LANES), vmem(2, 2, 8, LANES), vmem(2, 2, 8, LANES), vmem(2, 2, 8, LANES), vmem(2, 2, 8, LANES),
            vmem(5, 13, 5, 4, LANES), vmem(*low), vmem(*low), vmem(*low), vmem(2, *low), vmem(*low),
            vmem(3, 1, 40, LANES), vmem(4, LANES),
            vmem(3, MAXDEG, 2, 8, LANES),
            pltpu.SemaphoreType.DMA((MESSAGES,)), pltpu.SemaphoreType.DMA((MESSAGES,)),
        ],
        compiler_params=pltpu.CompilerParams(
            collective_id=0, has_side_effects=True, vmem_limit_bytes=56 * 1024 * 1024
        ),
    )(right_side, scale_field, mass_field, degrees, lower_bound, upper_bound)


def solution(mesh):
    cut = P("slab", "level", None)
    return jax.shard_map(
        shards, mesh=mesh, in_specs=(cut, cut, cut, P(), P(), P()), out_specs=(cut, cut), check_vma=False
    )
```

time: 1120 us -> 107 us (0.10)
  starting transfers between devices: 495 us -> 0 us
  waiting for transfers between devices: 448 us -> 0 us
  Pallas kernels: 0 us -> 104 us
  local copies, waits for them, and re-layouts: 88.1 us -> 2.26 us
  loops' own time: 38.7 us -> 0 us
  other arithmetic: 37.7 us -> 0 us
    ppermute x192 -> x0, starting transfers between devices: 495 us -> none  [the longest x96 302 us: extended(): before = lax.ppermute(last, axis, up)]
    ppermute x192 -> x0, waiting for transfers between devices: 448 us -> none  [the longest x96 448 us: extended(): before = lax.ppermute(last, axis, up)]
    pallas_call x0 -> x1, Pallas kernels: none -> 104 us  [shards(): pl.pallas_call(kernel, out_shape=(block, block), in_specs=[whole] * 3 + [...]
    reshape x8 -> x0, local copies, waits for them, and re-layouts: 70.4 us -> none  [the longest x5 49.5 us: average_cells(): blocks = field.reshape(size_z // 2, 2, size_x // 2, 2, size_y // 2, 2)]
    another operation x9 -> x0, loops' own time: 38.7 us -> none  [smooth(): result = lax.fori_loop(1, MAXDEG, sweep_turn, start_state)]
    reduce_sum x12 -> x0, other arithmetic: 20.9 us -> none  [average_cells(): return jnp.mean(blocks, axis=(1, 3, 5))]
    broadcast_in_dim x9 -> x0, local copies, waits for them, and re-layouts: 12.8 us -> none  [prolong(): jnp.broadcast_to(field[:, None, :, None, :, None], (size_z, 2, size_x, 2,...]
  transfers between devices with their start and end apart: 192 -> 0, of which waited for: 97 -> 0; matrix products, arithmetic and copies ran while one was open for 0% -> 0% of each run, Pallas kernels for 0% -> 0%
where the time goes in v1:
time: 107 us
  Pallas kernels  104 us (97%)
  local copies, waits for them, and re-layouts  2.26 us (2%)
    pallas_call x1, Pallas kernels, shards(): pl.pallas_call(kernel, out_shape=(block, block), in_specs=[whole] * 3 + [...  104 us
    unnamed x4, local copies, waits for them, and re-layouts  2.26 us

profile of v1, /device:TPU:6, one launch (start us, length us, event | category | flops | bytes accessed | tf_op | source)
XLA Modules:
  0.0 107.2 jit_solution(4187979582831220897)
XLA Ops:
  0.6 104.3 %shard_map.77 = (f32[4,16,512]{2,1,0:T(8,128)}, f32[4,16,512]{2,1,0:T(8,128)}) custom-call(f32[4,16,512]{2,1,0:T(8,128)} %rhs.1, f32[4,16,512]{2,1,0:T(8,128)} %scale.1, f32[4,16,512]{2,1,0:T(8,128)} %mass.1, s32[3]{0:T(128)} %degrees.1, f32[3]{0:T(128)} %lower.1, f32[3]{0:T(128)} %upper.1), custom_call_target="tpu_custom_call" | custom-call | tf_op jit(solution)/shard_map/pallas_call | solution.py:381
  104.9 0.0 copy-start
  104.9 1.6 %copy.10 = f32[4,16,512]{2,1,0:T(8,128)} copy(f32[4,16,512]{2,1,0:T(8,128)} %get-tuple-element.4) | data formatting | bytes 262144
  106.5 0.0 copy-done
  106.5 0.7 copy.11
Async XLA Ops:
  104.9 1.6 %copy-start = (f32[4,16,512]{2,1,0:T(8,128)S(1)}, f32[4,16,512]{2,1,0:T(8,128)}, u32[]{:S(2)}) copy-start(f32[4,16,512]{2,1,0:T(8,128)} %get-tuple-element.5) | copy-start | bytes 393220

commit v2 on v1

v2 whole, which is shorter than its diff:
```python
import jax
import jax.numpy as jnp
from jax import lax
from jax.experimental import pallas as pl
from jax.experimental.pallas import tpu as pltpu
from jax.sharding import PartitionSpec as P

CYCLES = 3
MAXDEG = 6
DEPTH = 6
UNROLL = True
PEERS = 16
LANES = 128
MESH = pl.DeviceIdType.MESH
f32 = jnp.float32
bf16 = jnp.bfloat16


def split_matrices():
    row = lax.broadcasted_iota(jnp.int32, (LANES, LANES), 0)
    col = lax.broadcasted_iota(jnp.int32, (LANES, LANES), 1)
    spread = [jnp.where(row == half * 64 + col // 2, 1.0, 0.0) for half in (0, 1)]
    gather = [jnp.where(col == half * 64 + row // 2, 1.0, 0.0) for half in (0, 1)]
    return jnp.concatenate(spread, axis=1).astype(bf16), jnp.concatenate(gather, axis=0).astype(bf16)


def dot(a, chosen):
    total = None
    for part in range(3):
        piece = a.astype(bf16)
        a = a - piece.astype(f32)
        product = jnp.dot(piece, chosen, preferred_element_type=f32)
        total = product if total is None else total + product
    return total


def kernel(
    rhs, scale, mass, degrees, lower, upper, sol_out, res_out,
    gf, kf, cf, wf, df, sf, pf, jf, tmp_c, tmp_q, tmp_r,
    gm, km, im, wm, dm, pm, jm, mid_c, mid_q, mid_r,
    lb, gl, kl, il, wl, dl, jl,
    coef, send_sem, recv_sem, cycle_send, cycle_recv,
):
    s = lax.axis_index("slab")
    l = lax.axis_index("level")
    once, every = [], []

    def clear(refs, first, planes, rows):
        for ref in refs:
            for z in range(first, first + planes):
                for t in range(ref.shape[1]):
                    ref[z, t, pl.ds(*rows), :] = jnp.zeros((rows[1], LANES), f32)

    fine_refs = [gf.at[0], gf.at[1], gf.at[2], kf, cf]
    mid_refs = [gm.at[0], gm.at[1], gm.at[2], km, im]
    low_refs = [lb.at[kind] for kind in range(5)]

    @pl.when(s < 6)
    def _():
        clear(fine_refs, 0, 6, (8, 32))
        clear(mid_refs, 0, 6, (8, 24))
        clear(low_refs, 0, 6, (0, 4))

    @pl.when(s > 9)
    def _():
        clear(fine_refs, 10, 6, (8, 32))
        clear(mid_refs, 8, 6, (8, 24))
        clear(low_refs, 7, 6, (0, 4))

    @pl.when(l < 2)
    def _():
        clear(fine_refs, 0, 16, (8, 8))
        clear(mid_refs, 0, 14, (8, 8))
        clear([ref.at[:, pl.ds(0, 2)] for ref in low_refs], 0, 13, (0, 4))

    @pl.when(l > 13)
    def _():
        clear(fine_refs, 0, 16, (32, 8))
        clear(mid_refs, 0, 14, (24, 8))
        clear([ref.at[:, pl.ds(3, 2)] for ref in low_refs], 0, 13, (0, 4))

    barrier = pltpu.get_barrier_semaphore()
    for step in range(1, 7):
        for sign in (1, -1):
            @pl.when((s + sign * step >= 0) & (s + sign * step < PEERS))
            def _(step=step, sign=sign):
                pl.semaphore_signal(barrier, inc=1, device_id={"slab": s + sign * step, "level": l}, device_id_type=MESH)
    for step in range(1, 3):
        for sign in (1, -1):
            @pl.when((l + sign * step >= 0) & (l + sign * step < PEERS))
            def _(step=step, sign=sign):
                pl.semaphore_signal(barrier, inc=1, device_id={"slab": s, "level": l + sign * step}, device_id_type=MESH)

    for hop in (2, -2):
        for step in (1, -1):
            @pl.when((s + hop >= 0) & (s + hop < PEERS) & (l + step >= 0) & (l + step < PEERS))
            def _(hop=hop, step=step):
                pl.semaphore_signal(barrier, inc=1, device_id={"slab": s + hop, "level": l + step}, device_id_type=MESH)

    class Message:
        def __init__(self, src, dst, ds=0, dl=0, cycle=None):
            kept = once if cycle is None else every
            self.at = len(kept)
            kept.append(self)
            self.src, self.dst, self.ds, self.dl, self.cycle = src, dst, ds, dl, cycle

        def copy(self):
            if self.cycle is None:
                send, recv = send_sem.at[self.at], recv_sem.at[self.at]
            else:
                send, recv = cycle_send.at[self.cycle].at[self.at], cycle_recv.at[self.cycle].at[self.at]
            return pltpu.make_async_remote_copy(
                src_ref=self.src, dst_ref=self.dst, send_sem=send, recv_sem=recv,
                device_id={"slab": s + self.ds, "level": l + self.dl}, device_id_type=MESH,
            )

        def valid(self, sign):
            inside = []
            for at, step in ((s, sign * self.ds), (l, sign * self.dl)):
                if step > 0:
                    inside.append(at < PEERS - step)
                elif step < 0:
                    inside.append(at >= -step)
            return inside[0] & inside[1] if len(inside) == 2 else inside[0]

        def start(self):
            @pl.when(self.valid(1))
            def _():
                self.copy().start()

        def arrived(self):
            @pl.when(self.valid(-1))
            def _():
                self.copy().wait_recv()

        def sent(self):
            @pl.when(self.valid(1))
            def _():
                self.copy().wait_send()

    def start(messages):
        for m in messages:
            m.start()
        return messages

    def arrived(messages):
        for m in messages:
            m.arrived()

    def z_messages(view, own, depth, hop, cycle=None):
        layers = max(0, min(own, depth - own * (hop - 1)))
        if layers == 0:
            return []
        gap = own * (hop - 1)
        top, bottom = 6 + own, 6
        return [
            Message(view(top - layers, layers), view(6 - gap - layers, layers), ds=hop, cycle=cycle),
            Message(view(bottom, layers), view(top + gap, layers), ds=-hop, cycle=cycle),
        ]

    def far_messages(buf, layers, cycle=None):
        result = []
        for ds, src, dst in ((2, 10 - layers, 2 - layers), (-2, 6, 14)):
            for dl, row, to, rows in ((0, 16, 16, 16), (1, 24, 8, 8), (-1, 16, 32, 8)):
                cut = lambda first, at: buf.at[pl.ds(first, layers), :, pl.ds(at, rows), :]
                result.append(Message(cut(src, row), cut(dst, to), ds=ds, dl=dl, cycle=cycle))
        return result

    def x_messages(buf, first, planes, width, cycle=None):
        cut = lambda row: buf.at[pl.ds(first, planes), :, pl.ds(row, 8), :]
        return [
            Message(cut(16 + width - 8), cut(8), dl=1, cycle=cycle),
            Message(cut(16), cut(16 + width), dl=-1, cycle=cycle),
        ]

    def low_x_messages(kind, depth, cycle=None):
        cut = lambda block: lb.at[kind].at[pl.ds(6 - depth, 1 + 2 * depth), block]
        return [Message(cut(2), cut(2 - step), dl=step, cycle=cycle) for step in (1, -1, 2, -2)]

    fine_view = lambda buf: (lambda first, layers: buf.at[pl.ds(first, layers), :, pl.ds(16, 16), :])
    mid_view = lambda buf: (lambda first, layers: buf.at[pl.ds(first, layers), :, pl.ds(16, 8), :])
    low_view = lambda kind: (lambda first, layers: lb.at[kind].at[pl.ds(first, layers), 2])

    for grid in range(3):
        low_b = jnp.full((8, LANES), lower[grid], f32)
        high_b = jnp.full((8, LANES), upper[grid], f32)
        degree = jnp.full((8, LANES), degrees[grid], jnp.int32)
        centre = (high_b + low_b) * 0.5
        radius = (high_b - low_b) * 0.5
        ratio = centre / radius
        rho = 1.0 / ratio
        coef[grid, 0, 0] = 1.0 / centre
        for j in range(1, MAXDEG):
            rho_new = 1.0 / (2.0 * ratio - rho)
            active = j < degree
            coef[grid, j, 0] = jnp.where(active, rho_new * rho, 0.0)
            coef[grid, j, 1] = jnp.where(active, 2.0 * rho_new / radius, 0.0)
            rho = rho_new

    spread, gather = split_matrices()
    lane = lax.broadcasted_iota(jnp.int32, (1, LANES), 1)

    def tile_rows(v, rows):
        return jnp.concatenate([v] * (rows // 8), axis=0) if rows > 8 else v

    def x_sum(ref, z, tiles, r0, rows):
        return tuple(
            ref[z, t, pl.ds(r0 - 1, rows), :] + ref[z, t, pl.ds(r0, rows), :] + ref[z, t, pl.ds(r0 + 1, rows), :]
            for t in range(tiles)
        )

    def y_sum(vals):
        right = [pltpu.roll(v, 1, 1) for v in vals]
        left = [pltpu.roll(v, LANES - 1, 1) for v in vals]
        out = []
        for t, v in enumerate(vals):
            before = right[t - 1] if t > 0 else 0.0
            after = left[t + 1] if t + 1 < len(vals) else 0.0
            out.append(v + jnp.where(lane == 0, before, right[t]) + jnp.where(lane == LANES - 1, after, left[t]))
        return out

    def sweep(src, lo, hi, tiles, r0, rows, use, whole=True):
        first = (x_sum(src, lo - 1, tiles, r0, rows), x_sum(src, lo, tiles, r0, rows))

        def plane(z, carry):
            below, here = carry
            above = x_sum(src, z + 1, tiles, r0, rows)
            box = y_sum([a + b + c for a, b, c in zip(below, here, above)])
            use(z, box)
            return here, above

        if whole:
            carry = first
            for z in range(lo, hi):
                carry = plane(z, carry)
        else:
            lax.fori_loop(lo, hi, plane, first, unroll=(hi - lo) // 2)

    def smooth(grid, g, k, w, d, own, tiles, chunks):
        planes = own + 2 * DEPTH
        for j in range(1, MAXDEG):
            new = w.at[(j - 1) % 2]
            old = g if j == 1 else w.at[j % 2]
            for r0, rows in chunks:
                a = tile_rows(coef[grid, j, 0], rows)
                b = tile_rows(coef[grid, j, 1], rows)
                first = tile_rows(coef[grid, 0, 0], rows)

                def use(z, box, j=j, r0=r0, rows=rows, a=a, b=b, first=first, new=new, old=old):
                    cut = pl.ds(r0, rows)
                    for t in range(tiles):
                        source = g[z, t, cut, :]
                        if j == 1:
                            here = source * first
                            total = box[t] * first
                            direction = here
                        else:
                            here = old[z, t, cut, :]
                            total = box[t]
                            direction = d[z, t, cut, :]
                        defect = (source - here) + k[z, t, cut, :] * (total - here)
                        direction = a * direction + b * defect
                        d[z, t, cut, :] = direction
                        new[z, t, cut, :] = here + direction

                sweep(old, j, planes - j, tiles, r0, rows, use, whole=UNROLL or grid > 0)

    def restrict(src, planes, tiles, rows):
        sums = []
        for z in range(planes // 2):
            for t in range(tiles):
                total = None
                for dz in (0, 1):
                    for dx in (0, 1):
                        part = src[2 * z + dz, t, pl.ds(dx, rows, stride=2), :]
                        total = part if total is None else total + part
                sums.append(total * 0.125)
        pairs = [jnp.concatenate(sums[at:at + 2], axis=1) for at in range(0, len(sums), 2)]
        joined = dot(jnp.concatenate(pairs, axis=0), gather)
        half = tiles // 2
        return [
            [joined[rows * (z * half + o):rows * (z * half + o + 1)] for o in range(half)] for z in range(planes // 2)
        ]

    for z in range(4):
        for t in range(4):
            cut = pl.ds(t * LANES, LANES)
            c = scale[z, :, cut]
            q = mass[z, :, cut]
            diag = c * c + q
            inverse = 1.0 / diag
            tmp_c[z, t] = c
            tmp_q[z, t] = q
            jf[z, t] = diag / c
            b = rhs[z, :, cut]
            tmp_r[z, t] = b
            kf[6 + z, t, pl.ds(16, 16), :] = c * c * inverse * (1.0 / 26.0)
            cf[6 + z, t, pl.ds(16, 16), :] = c
            gf[0, 6 + z, t, pl.ds(16, 16), :] = c * inverse * b

    up, down = jnp.minimum(s, 6), jnp.minimum(PEERS - 1 - s, 6)
    left, right = jnp.minimum(l, 2), jnp.minimum(PEERS - 1 - l, 2)
    corners = (jnp.minimum(up // 2, 1) + jnp.minimum(down // 2, 1)) * (jnp.minimum(left, 1) + jnp.minimum(right, 1))
    greet = up + down + left + right + corners
    pl.semaphore_wait(barrier, greet)

    for z in range(5, 11):
        for t in range(4):
            sf[z, t, pl.ds(8, 32), :] = jnp.zeros((32, LANES), f32)

    shallow = DEPTH - 1
    near_k = z_messages(fine_view(kf), 4, shallow, 1) + z_messages(fine_view(cf), 4, 1, 1)
    side_k = x_messages(kf, 6, 4, 16)
    far_k = far_messages(kf, shallow - 4)
    low_zk, mid_zk = [], []
    for hop in range(1, 7):
        low_zk += z_messages(low_view(3), 1, shallow, hop) + z_messages(low_view(4), 1, 1, hop)
    for hop in range(1, 4):
        mid_zk += z_messages(mid_view(km), 2, shallow, hop) + z_messages(mid_view(im), 2, 1, hop)
    low_xk = low_x_messages(3, shallow) + low_x_messages(4, 1)
    mid_xk = x_messages(km, 1, 12, 8) + x_messages(im, 5, 4, 8)
    relay_k = x_messages(kf, 2, 4, 16) + x_messages(kf, 10, 4, 16) + x_messages(cf, 5, 6, 16)

    def cycle_body(cycle, carry):
        opening = pl.when(cycle == 0)
        g = gf.at[cycle]
        near = z_messages(fine_view(g), 4, DEPTH, 1, cycle)
        side = x_messages(g, 6, 4, 16, cycle)
        far = far_messages(g, DEPTH - 4, cycle)
        start(near)
        start(side)

        @opening
        def _():
            start(near_k)
            start(side_k)
            cs, qs = restrict(tmp_c, 4, 4, 8), restrict(tmp_q, 4, 4, 8)
            for z in range(2):
                for t in range(2):
                    c, q = cs[z][t], qs[z][t]
                    diag = c * c + q
                    mid_c[z, t] = c
                    mid_q[z, t] = q
                    jm[z, t] = c / diag
                    km[6 + z, t, pl.ds(16, 8), :] = c * c / diag * (1.0 / 26.0)
                    im[6 + z, t, pl.ds(16, 8), :] = 1.0 / c
            c, q = restrict(mid_c, 2, 2, 4)[0][0], restrict(mid_q, 2, 2, 4)[0][0]
            diag = c * c + q
            jl[...] = c / diag
            lb[3, 6, 2] = c * c / diag * (1.0 / 26.0)
            lb[4, 6, 2] = 1.0 / c

        rs = restrict(tmp_r, 4, 4, 8)
        for z in range(2):
            for t in range(2):
                r = 4.0 * rs[z][t]
                mid_r[z, t] = r
                gm[cycle, 6 + z, t, pl.ds(16, 8), :] = r * jm[z, t]
        lb[cycle, 6, 2] = 4.0 * restrict(mid_r, 2, 2, 4)[0][0] * jl[...]

        low_z, mid_z = [], []
        for hop in range(1, 7):
            low_z += z_messages(low_view(cycle), 1, DEPTH, hop, cycle)
        for hop in range(1, 4):
            mid_z += z_messages(mid_view(gm.at[cycle]), 2, DEPTH, hop, cycle)
        low_x = low_x_messages(cycle, DEPTH, cycle)
        mid_x = x_messages(gm.at[cycle], 0, 14, 8, cycle)
        relay = x_messages(g, 2, 4, 16, cycle) + x_messages(g, 10, 4, 16, cycle)
        start(low_z)
        start(mid_z)
        start(far)

        @opening
        def _():
            start(low_zk)
            start(mid_zk)
            start(far_k)

        arrived(near)
        start(relay)

        @opening
        def _():
            arrived(near_k)
            start(relay_k)

        arrived(low_z)
        start(low_x)
        arrived(mid_z)
        start(mid_x)

        @opening
        def _():
            arrived(low_zk)
            start(low_xk)
            arrived(mid_zk)
            start(mid_xk)

        arrived(low_x)

        @opening
        def _():
            arrived(low_xk)
            for kind, dst in ((3, kl), (4, il)):
                for block in range(5):
                    dst[:, 0, pl.ds(6 + 4 * block, 4), :] = lb[kind, :, block]

        for block in range(5):
            gl[:, 0, pl.ds(6 + 4 * block, 4), :] = lb[cycle, :, block]
        smooth(2, gl, kl, wl, dl, 1, 1, [(8, 16)])
        cut = pl.ds(12, 8)
        coarse = jnp.concatenate([wl[0, z, 0, cut, :] * il[z, 0, cut, :] for z in range(5, 8)], axis=0)
        wide = dot(coarse, spread)
        for z in range(3):
            for t in range(2):
                for dx in (0, 1):
                    pm[z, t, pl.ds(dx, 8, stride=2), :] = wide[8 * z:8 * z + 8, t * LANES:(t + 1) * LANES]

        arrived(mid_x)
        opening(lambda: arrived(mid_xk))
        smooth(1, gm.at[cycle], km, wm, dm, 2, 2, [(8, 24)])
        cut = pl.ds(12, 16)
        coarse = jnp.concatenate([
            wm[0, z, t, cut, :] * im[z, t, cut, :] + pm[(z - 6) // 2 + 1, t]
            for z in range(5, 9) for t in range(2)
        ], axis=0)
        wide = dot(coarse, spread)
        for z in range(4):
            for t in range(4):
                row, half = 16 * (2 * z + t // 2), t % 2
                for dx in (0, 1):
                    pf[z, t, pl.ds(dx, 16, stride=2), :] = wide[row:row + 16, half * LANES:(half + 1) * LANES]

        arrived(far)
        arrived(side + relay)
        opening(lambda: arrived(far_k + side_k + relay_k))
        smooth(0, g, kf, wf, df, 4, 4, [(8, 16), (24, 16)])
        for z in range(5, 11):
            for t in range(4):
                cut = pl.ds(8, 32)
                step = 0.5 * (wf[0, z, t, cut, :] + cf[z, t, cut, :] * pf[(z - 6) // 2 + 1, t])
                sf[z, t, cut, :] += step

        def residual(z, box):
            cut = pl.ds(16, 16)
            for t in range(4):
                here = sf[z, t, cut, :]
                scaled = gf[0, z, t, cut, :] - here + kf[z, t, cut, :] * (box[t] - here)
                plain = scaled * jf[z - 6, t]
                gf[cycle + 1, z, t, cut, :] = scaled
                tmp_r[z - 6, t] = plain
                out = pl.ds(t * LANES, LANES)
                sol_out[z - 6, :, out] = here / cf[z, t, cut, :]
                res_out[z - 6, :, out] = plain

        sweep(sf, 6, 10, 4, 16, 16, residual)
        for m in every:
            m.sent()
        return carry

    lax.fori_loop(0, CYCLES, cycle_body, 0)
    assert len(once) <= ONCE and len(every) <= EVERY
    for m in once:
        m.sent()


ONCE, EVERY = 80, 48


def shards(right_side, scale_field, mass_field, degrees, lower_bound, upper_bound):
    vmem = lambda *dims: pltpu.VMEM(dims, f32)
    fine, mid, low = (16, 4, 48, LANES), (14, 2, 40, LANES), (13, 1, 40, LANES)
    block = jax.ShapeDtypeStruct(right_side.shape, f32)
    whole = pl.BlockSpec(memory_space=pltpu.VMEM)
    scalar = pl.BlockSpec(memory_space=pltpu.SMEM)
    return pl.pallas_call(
        kernel,
        out_shape=(block, block),
        in_specs=[whole] * 3 + [scalar] * 3,
        out_specs=(whole, whole),
        scratch_shapes=[
            vmem(4, *fine), vmem(*fine), vmem(*fine), vmem(2, *fine), vmem(*fine), vmem(*fine),
            vmem(4, 4, 32, LANES), vmem(4, 4, 16, LANES), vmem(4, 4, 16, LANES), vmem(4, 4, 16, LANES), vmem(4, 4, 16, LANES),
            vmem(3, *mid), vmem(*mid), vmem(*mid), vmem(2, *mid), vmem(*mid),
            vmem(3, 2, 16, LANES), vmem(2, 2, 8, LANES), vmem(2, 2, 8, LANES), vmem(2, 2, 8, LANES), vmem(2, 2, 8, LANES),
            vmem(5, 13, 5, 4, LANES), vmem(*low), vmem(*low), vmem(*low), vmem(2, *low), vmem(*low),
            vmem(4, LANES),
            vmem(3, MAXDEG, 2, 8, LANES),
            pltpu.SemaphoreType.DMA((ONCE,)), pltpu.SemaphoreType.DMA((ONCE,)),
            pltpu.SemaphoreType.DMA((CYCLES, EVERY)), pltpu.SemaphoreType.DMA((CYCLES, EVERY)),
        ],
        compiler_params=pltpu.CompilerParams(
            collective_id=0, has_side_effects=True, vmem_limit_bytes=56 * 1024 * 1024
        ),
    )(right_side, scale_field, mass_field, degrees, lower_bound, upper_bound)


def solution(mesh):
    cut = P("slab", "level", None)
    return jax.shard_map(
        shards, mesh=mesh, in_specs=(cut, cut, cut, P(), P(), P()), out_specs=(cut, cut), check_vma=False
    )
```

time: 107 us -> 89 us (0.83)
  Pallas kernels: 104 us -> 85.9 us
    pallas_call x1, Pallas kernels: 104 us -> 85.9 us  [shards(): pl.pallas_call(kernel, out_shape=(block, block), in_specs=[whole] * 3 + [...]
where the time goes in v2:
time: 89 us; the launch traced here: 88.8 us
  Pallas kernels  85.9 us (97%)
  local copies, waits for them, and re-layouts  2.26 us (3%)
    pallas_call x1, Pallas kernels, shards(): pl.pallas_call(kernel, out_shape=(block, block), in_specs=[whole] * 3 + [...  85.9 us
    unnamed x4, local copies, waits for them, and re-layouts  2.26 us

profile of v2, /device:TPU:6, one launch (start us, length us, event | category | flops | bytes accessed | tf_op | source)
XLA Modules:
  0.0 88.8 jit_solution(4477011544150932434)
XLA Ops:
  0.6 85.9 %shard_map.77 = (f32[4,16,512]{2,1,0:T(8,128)}, f32[4,16,512]{2,1,0:T(8,128)}) custom-call(f32[4,16,512]{2,1,0:T(8,128)} %rhs.1, f32[4,16,512]{2,1,0:T(8,128)} %scale.1, f32[4,16,512]{2,1,0:T(8,128)} %mass.1, s32[3]{0:T(128)} %degrees.1, f32[3]{0:T(128)} %lower.1, f32[3]{0:T(128)} %upper.1), custom_call_target="tpu_custom_call" | custom-call | tf_op jit(solution)/shard_map/pallas_call | solution.py:476
  86.6 0.0 copy-start
  86.6 1.6 %copy.10 = f32[4,16,512]{2,1,0:T(8,128)} copy(f32[4,16,512]{2,1,0:T(8,128)} %get-tuple-element.4) | data formatting | bytes 262144
  88.2 0.0 copy-done
  88.2 0.7 copy.11
Async XLA Ops:
  86.6 1.6 %copy-start = (f32[4,16,512]{2,1,0:T(8,128)S(1)}, f32[4,16,512]{2,1,0:T(8,128)}, u32[]{:S(2)}) copy-start(f32[4,16,512]{2,1,0:T(8,128)} %get-tuple-element.5) | copy-start | bytes 393220

commit v3 on v2

--- a/solution.py
+++ b/solution.py
@@ -8,7 +8,6 @@
 CYCLES = 3
 MAXDEG = 6
 DEPTH = 6
-UNROLL = True
 PEERS = 16
 LANES = 128
 MESH = pl.DeviceIdType.MESH
@@ -35,15 +34,22 @@
 
 
 def kernel(
-    rhs, scale, mass, degrees, lower, upper, sol_out, res_out,
+    rhs_in, scale_in, mass_in, degrees, lower, upper, sol_out, res_out,
+    rhs, scale, mass,
     gf, kf, cf, wf, df, sf, pf, jf, tmp_c, tmp_q, tmp_r,
     gm, km, im, wm, dm, pm, jm, mid_c, mid_q, mid_r,
     lb, gl, kl, il, wl, dl, jl,
-    coef, send_sem, recv_sem, cycle_send, cycle_recv,
+    coef, load_sem, send_sem, recv_sem, cycle_send, cycle_recv,
 ):
     s = lax.axis_index("slab")
     l = lax.axis_index("level")
     once, every = [], []
+    loads = [
+        pltpu.make_async_copy(src, dst, load_sem.at[i])
+        for i, (src, dst) in enumerate(((scale_in, scale), (mass_in, mass), (rhs_in, rhs)))
+    ]
+    for load in loads:
+        load.start()
 
     def clear(refs, first, planes, rows):
         for ref in refs:
@@ -91,12 +97,6 @@
             def _(step=step, sign=sign):
                 pl.semaphore_signal(barrier, inc=1, device_id={"slab": s, "level": l + sign * step}, device_id_type=MESH)
 
-    for hop in (2, -2):
-        for step in (1, -1):
-            @pl.when((s + hop >= 0) & (s + hop < PEERS) & (l + step >= 0) & (l + step < PEERS))
-            def _(hop=hop, step=step):
-                pl.semaphore_signal(barrier, inc=1, device_id={"slab": s + hop, "level": l + step}, device_id_type=MESH)
-
     class Message:
         def __init__(self, src, dst, ds=0, dl=0, cycle=None):
             kept = once if cycle is None else every
@@ -114,38 +114,26 @@
                 device_id={"slab": s + self.ds, "level": l + self.dl}, device_id_type=MESH,
             )
 
-        def valid(self, sign):
-            inside = []
-            for at, step in ((s, sign * self.ds), (l, sign * self.dl)):
-                if step > 0:
-                    inside.append(at < PEERS - step)
-                elif step < 0:
-                    inside.append(at >= -step)
-            return inside[0] & inside[1] if len(inside) == 2 else inside[0]
-
-        def start(self):
-            @pl.when(self.valid(1))
-            def _():
-                self.copy().start()
-
-        def arrived(self):
-            @pl.when(self.valid(-1))
-            def _():
-                self.copy().wait_recv()
-
-        def sent(self):
-            @pl.when(self.valid(1))
-            def _():
-                self.copy().wait_send()
+    def by_partner(messages, sign, act):
+        groups = {}
+        for m in messages:
+            groups.setdefault((sign * m.ds, sign * m.dl), []).append(m)
+        for (ds, dl), group in groups.items():
+            at, step = (s, ds) if ds else (l, dl)
+
+            @pl.when(at < PEERS - step if step > 0 else at >= -step)
+            def _(group=group):
+                for m in group:
+                    act(m)
 
     def start(messages):
-        for m in messages:
-            m.start()
-        return messages
+        by_partner(messages, 1, lambda m: m.copy().start())
 
     def arrived(messages):
-        for m in messages:
-            m.arrived()
+        by_partner(messages, -1, lambda m: m.copy().wait_recv())
+
+    def sent(messages):
+        by_partner(messages, 1, lambda m: m.copy().wait_send())
 
     def z_messages(view, own, depth, hop, cycle=None):
         layers = max(0, min(own, depth - own * (hop - 1)))
@@ -158,18 +146,10 @@
             Message(view(bottom, layers), view(top + gap, layers), ds=-hop, cycle=cycle),
         ]
 
-    def far_messages(buf, layers, cycle=None):
-        result = []
-        for ds, src, dst in ((2, 10 - layers, 2 - layers), (-2, 6, 14)):
-            for dl, row, to, rows in ((0, 16, 16, 16), (1, 24, 8, 8), (-1, 16, 32, 8)):
-                cut = lambda first, at: buf.at[pl.ds(first, layers), :, pl.ds(at, rows), :]
-                result.append(Message(cut(src, row), cut(dst, to), ds=ds, dl=dl, cycle=cycle))
-        return result
-
     def x_messages(buf, first, planes, width, cycle=None):
-        cut = lambda row: buf.at[pl.ds(first, planes), :, pl.ds(row, 8), :]
+        cut = lambda row: buf.at[pl.ds(first, planes), :, pl.ds(row, 6), :]
         return [
-            Message(cut(16 + width - 8), cut(8), dl=1, cycle=cycle),
+            Message(cut(16 + width - 6), cut(10), dl=1, cycle=cycle),
             Message(cut(16), cut(16 + width), dl=-1, cycle=cycle),
         ]
 
@@ -219,7 +199,7 @@
             out.append(v + jnp.where(lane == 0, before, right[t]) + jnp.where(lane == LANES - 1, after, left[t]))
         return out
 
-    def sweep(src, lo, hi, tiles, r0, rows, use, whole=True):
+    def sweep(src, lo, hi, tiles, r0, rows, use):
         first = (x_sum(src, lo - 1, tiles, r0, rows), x_sum(src, lo, tiles, r0, rows))
 
         def plane(z, carry):
@@ -229,24 +209,21 @@
             use(z, box)
             return here, above
 
-        if whole:
-            carry = first
-            for z in range(lo, hi):
-                carry = plane(z, carry)
-        else:
-            lax.fori_loop(lo, hi, plane, first, unroll=(hi - lo) // 2)
-
-    def smooth(grid, g, k, w, d, own, tiles, chunks):
+        for z in range(lo, hi):
+            first = plane(z, first)
+
+    def smooth(grid, g, k, w, d, own, tiles, chunks, spans=None):
         planes = own + 2 * DEPTH
         for j in range(1, MAXDEG):
-            new = w.at[(j - 1) % 2]
-            old = g if j == 1 else w.at[j % 2]
-            for r0, rows in chunks:
+            new, turn = w.at[j - 1], d.at[j - 1]
+            old, past = (g, None) if j == 1 else (w.at[j - 2], d.at[j - 2])
+            parts = [(j, planes - j)] if spans is None else spans(j)
+            for (r0, rows), (lo, hi) in [(chunk, part) for chunk in chunks for part in parts]:
                 a = tile_rows(coef[grid, j, 0], rows)
                 b = tile_rows(coef[grid, j, 1], rows)
                 first = tile_rows(coef[grid, 0, 0], rows)
 
-                def use(z, box, j=j, r0=r0, rows=rows, a=a, b=b, first=first, new=new, old=old):
+                def use(z, box, j=j, r0=r0, rows=rows, a=a, b=b, first=first, new=new, old=old, turn=turn, past=past):
                     cut = pl.ds(r0, rows)
                     for t in range(tiles):
                         source = g[z, t, cut, :]
@@ -257,13 +234,13 @@
                         else:
                             here = old[z, t, cut, :]
                             total = box[t]
-                            direction = d[z, t, cut, :]
+                            direction = past[z, t, cut, :]
                         defect = (source - here) + k[z, t, cut, :] * (total - here)
                         direction = a * direction + b * defect
-                        d[z, t, cut, :] = direction
+                        turn[z, t, cut, :] = direction
                         new[z, t, cut, :] = here + direction
 
-                sweep(old, j, planes - j, tiles, r0, rows, use, whole=UNROLL or grid > 0)
+                sweep(old, lo, hi, tiles, r0, rows, use)
 
     def restrict(src, planes, tiles, rows):
         sums = []
@@ -282,6 +259,8 @@
             [joined[rows * (z * half + o):rows * (z * half + o + 1)] for o in range(half)] for z in range(planes // 2)
         ]
 
+    for load in loads:
+        load.wait()
     for z in range(4):
         for t in range(4):
             cut = pl.ds(t * LANES, LANES)
@@ -300,9 +279,7 @@
 
     up, down = jnp.minimum(s, 6), jnp.minimum(PEERS - 1 - s, 6)
     left, right = jnp.minimum(l, 2), jnp.minimum(PEERS - 1 - l, 2)
-    corners = (jnp.minimum(up // 2, 1) + jnp.minimum(down // 2, 1)) * (jnp.minimum(left, 1) + jnp.minimum(right, 1))
-    greet = up + down + left + right + corners
-    pl.semaphore_wait(barrier, greet)
+    pl.semaphore_wait(barrier, up + down + left + right)
 
     for z in range(5, 11):
         for t in range(4):
@@ -311,7 +288,8 @@
     shallow = DEPTH - 1
     near_k = z_messages(fine_view(kf), 4, shallow, 1) + z_messages(fine_view(cf), 4, 1, 1)
     side_k = x_messages(kf, 6, 4, 16)
-    far_k = far_messages(kf, shallow - 4)
+    far_k = z_messages(fine_view(kf), 4, shallow, 2)
+    last_k = x_messages(kf, 1, 1, 16) + x_messages(kf, 14, 1, 16)
     low_zk, mid_zk = [], []
     for hop in range(1, 7):
         low_zk += z_messages(low_view(3), 1, shallow, hop) + z_messages(low_view(4), 1, 1, hop)
@@ -325,15 +303,20 @@
         opening = pl.when(cycle == 0)
         g = gf.at[cycle]
         near = z_messages(fine_view(g), 4, DEPTH, 1, cycle)
+        far = z_messages(fine_view(g), 4, DEPTH, 2, cycle)
         side = x_messages(g, 6, 4, 16, cycle)
-        far = far_messages(g, DEPTH - 4, cycle)
-        start(near)
-        start(side)
-
-        @opening
-        def _():
-            start(near_k)
-            start(side_k)
+        relay = x_messages(g, 2, 4, 16, cycle) + x_messages(g, 10, 4, 16, cycle)
+        last = x_messages(g, 0, 2, 16, cycle) + x_messages(g, 14, 2, 16, cycle)
+        low_z, mid_z = [], []
+        for hop in range(1, 7):
+            low_z += z_messages(low_view(cycle), 1, DEPTH, hop, cycle)
+        for hop in range(1, 4):
+            mid_z += z_messages(mid_view(gm.at[cycle]), 2, DEPTH, hop, cycle)
+        low_x = low_x_messages(cycle, DEPTH, cycle)
+        mid_x = x_messages(gm.at[cycle], 0, 14, 8, cycle)
+
+        @opening
+        def _():
             cs, qs = restrict(tmp_c, 4, 4, 8), restrict(tmp_q, 4, 4, 8)
             for z in range(2):
                 for t in range(2):
@@ -358,23 +341,51 @@
                 gm[cycle, 6 + z, t, pl.ds(16, 8), :] = r * jm[z, t]
         lb[cycle, 6, 2] = 4.0 * restrict(mid_r, 2, 2, 4)[0][0] * jl[...]
 
-        low_z, mid_z = [], []
-        for hop in range(1, 7):
-            low_z += z_messages(low_view(cycle), 1, DEPTH, hop, cycle)
-        for hop in range(1, 4):
-            mid_z += z_messages(mid_view(gm.at[cycle]), 2, DEPTH, hop, cycle)
-        low_x = low_x_messages(cycle, DEPTH, cycle)
-        mid_x = x_messages(gm.at[cycle], 0, 14, 8, cycle)
-        relay = x_messages(g, 2, 4, 16, cycle) + x_messages(g, 10, 4, 16, cycle)
         start(low_z)
+
+        @opening
+        def _():
+            start(low_zk)
+
         start(mid_z)
+
+        @opening
+        def _():
+            start(mid_zk)
+
+        start(near)
+
+        @opening
+        def _():
+            start(near_k)
+
+        start(side)
+
+        @opening
+        def _():
+            start(side_k)
+
         start(far)
 
         @opening
         def _():
-            start(low_zk)
-            start(mid_zk)
             start(far_k)
+
+        arrived(low_z)
+        start(low_x)
+
+        @opening
+        def _():
+            arrived(low_zk)
+            start(low_xk)
+
+        arrived(mid_z)
+        start(mid_x)
+
+        @opening
+        def _():
+            arrived(mid_zk)
+            start(mid_xk)
 
         arrived(near)
         start(relay)
@@ -384,17 +395,13 @@
             arrived(near_k)
             start(relay_k)
 
-        arrived(low_z)
-        start(low_x)
-        arrived(mid_z)
-        start(mid_x)
-
-        @opening
-        def _():
-            arrived(low_zk)
-            start(low_xk)
-            arrived(mid_zk)
-            start(mid_xk)
+        arrived(far)
+        start(last)
+
+        @opening
+        def _():
+            arrived(far_k)
+            start(last_k)
 
         arrived(low_x)
 
@@ -409,7 +416,7 @@
             gl[:, 0, pl.ds(6 + 4 * block, 4), :] = lb[cycle, :, block]
         smooth(2, gl, kl, wl, dl, 1, 1, [(8, 16)])
         cut = pl.ds(12, 8)
-        coarse = jnp.concatenate([wl[0, z, 0, cut, :] * il[z, 0, cut, :] for z in range(5, 8)], axis=0)
+        coarse = jnp.concatenate([wl[4, z, 0, cut, :] * il[z, 0, cut, :] for z in range(5, 8)], axis=0)
         wide = dot(coarse, spread)
         for z in range(3):
             for t in range(2):
@@ -421,7 +428,7 @@
         smooth(1, gm.at[cycle], km, wm, dm, 2, 2, [(8, 24)])
         cut = pl.ds(12, 16)
         coarse = jnp.concatenate([
-            wm[0, z, t, cut, :] * im[z, t, cut, :] + pm[(z - 6) // 2 + 1, t]
+            wm[4, z, t, cut, :] * im[z, t, cut, :] + pm[(z - 6) // 2 + 1, t]
             for z in range(5, 9) for t in range(2)
         ], axis=0)
         wide = dot(coarse, spread)
@@ -431,14 +438,19 @@
                 for dx in (0, 1):
                     pf[z, t, pl.ds(dx, 16, stride=2), :] = wide[row:row + 16, half * LANES:(half + 1) * LANES]
 
-        arrived(far)
         arrived(side + relay)
-        opening(lambda: arrived(far_k + side_k + relay_k))
-        smooth(0, g, kf, wf, df, 4, 4, [(8, 16), (24, 16)])
+        opening(lambda: arrived(side_k + relay_k))
+        chunks = [(8, 16), (24, 16)]
+        smooth(0, g, kf, wf, df, 4, 4, chunks, lambda j: [(2 + j, 14 - j)])
+
+        arrived(last)
+        opening(lambda: arrived(last_k))
+        smooth(0, g, kf, wf, df, 4, 4, chunks, lambda j: [(j, 2 + j), (14 - j, 16 - j)])
+
         for z in range(5, 11):
             for t in range(4):
                 cut = pl.ds(8, 32)
-                step = 0.5 * (wf[0, z, t, cut, :] + cf[z, t, cut, :] * pf[(z - 6) // 2 + 1, t])
+                step = 0.5 * (wf[4, z, t, cut, :] + cf[z, t, cut, :] * pf[(z - 6) // 2 + 1, t])
                 sf[z, t, cut, :] += step
 
         def residual(z, box):
@@ -454,14 +466,12 @@
                 res_out[z - 6, :, out] = plain
 
         sweep(sf, 6, 10, 4, 16, 16, residual)
-        for m in every:
-            m.sent()
+        sent(every)
         return carry
 
     lax.fori_loop(0, CYCLES, cycle_body, 0)
     assert len(once) <= ONCE and len(every) <= EVERY
-    for m in once:
-        m.sent()
+    sent(once)
 
 
 ONCE, EVERY = 80, 48
@@ -476,16 +486,18 @@
     return pl.pallas_call(
         kernel,
         out_shape=(block, block),
-        in_specs=[whole] * 3 + [scalar] * 3,
+        in_specs=[pl.BlockSpec(memory_space=pl.ANY)] * 3 + [scalar] * 3,
         out_specs=(whole, whole),
         scratch_shapes=[
-            vmem(4, *fine), vmem(*fine), vmem(*fine), vmem(2, *fine), vmem(*fine), vmem(*fine),
+            vmem(4, 16, 512), vmem(4, 16, 512), vmem(4, 16, 512),
+            vmem(4, *fine), vmem(*fine), vmem(*fine), vmem(5, *fine), vmem(5, *fine), vmem(*fine),
             vmem(4, 4, 32, LANES), vmem(4, 4, 16, LANES), vmem(4, 4, 16, LANES), vmem(4, 4, 16, LANES), vmem(4, 4, 16, LANES),
-            vmem(3, *mid), vmem(*mid), vmem(*mid), vmem(2, *mid), vmem(*mid),
+            vmem(3, *mid), vmem(*mid), vmem(*mid), vmem(5, *mid), vmem(5, *mid),
             vmem(3, 2, 16, LANES), vmem(2, 2, 8, LANES), vmem(2, 2, 8, LANES), vmem(2, 2, 8, LANES), vmem(2, 2, 8, LANES),
-            vmem(5, 13, 5, 4, LANES), vmem(*low), vmem(*low), vmem(*low), vmem(2, *low), vmem(*low),
+            vmem(5, 13, 5, 4, LANES), vmem(*low), vmem(*low), vmem(*low), vmem(5, *low), vmem(5, *low),
             vmem(4, LANES),
             vmem(3, MAXDEG, 2, 8, LANES),
+            pltpu.SemaphoreType.DMA((3,)),
             pltpu.SemaphoreType.DMA((ONCE,)), pltpu.SemaphoreType.DMA((ONCE,)),
             pltpu.SemaphoreType.DMA((CYCLES, EVERY)), pltpu.SemaphoreType.DMA((CYCLES, EVERY)),
         ],

time: 89 us -> 75.6 us (0.85)
  Pallas kernels: 85.9 us -> 71.8 us
    pallas_call x1, Pallas kernels: 85.9 us -> 71.8 us  [shards(): pl.pallas_call(kernel, out_shape=(block, block), in_specs=[pl.BlockSpec(m...]
where the time goes in v3:
time: 75.6 us; the launch traced here: 74.7 us
  Pallas kernels  71.8 us (95%)
  local copies, waits for them, and re-layouts  2.26 us (3%)
    pallas_call x1, Pallas kernels, shards(): pl.pallas_call(kernel, out_shape=(block, block), in_specs=[pl.BlockSpec(m...  71.8 us
    unnamed x4, local copies, waits for them, and re-layouts  2.26 us

profile of v3, /device:TPU:6, one launch (start us, length us, event | category | flops | bytes accessed | tf_op | source)
XLA Modules:
  0.0 74.7 jit_solution(9998946661123172791)
XLA Ops:
  0.6 71.8 %shard_map.77 = (f32[4,16,512]{2,1,0:T(8,128)}, f32[4,16,512]{2,1,0:T(8,128)}) custom-call(f32[4,16,512]{2,1,0:T(8,128)} %rhs_in.1, f32[4,16,512]{2,1,0:T(8,128)} %scale_in.1, f32[4,16,512]{2,1,0:T(8,128)} %mass_in.1, s32[3]{0:T(128)} %degrees.1, f32[3]{0:T(128)} %lower.1, f32[3]{0:T(128)} %upper.1), custom_call_target="tpu_custom_call" | custom-call | tf_op jit(solution)/shard_map/pallas_call | solution.py:486
  72.4 0.0 copy-start
  72.4 1.6 %copy.10 = f32[4,16,512]{2,1,0:T(8,128)} copy(f32[4,16,512]{2,1,0:T(8,128)} %get-tuple-element.4) | data formatting | bytes 262144
  74.0 0.0 copy-done
  74.1 0.7 copy.11
Async XLA Ops:
  72.4 1.6 %copy-start = (f32[4,16,512]{2,1,0:T(8,128)S(1)}, f32[4,16,512]{2,1,0:T(8,128)}, u32[]{:S(2)}) copy-start(f32[4,16,512]{2,1,0:T(8,128)} %get-tuple-element.5) | copy-start | bytes 393220

commit v4 on v3

--- a/solution.py
+++ b/solution.py
@@ -20,7 +20,8 @@
     col = lax.broadcasted_iota(jnp.int32, (LANES, LANES), 1)
     spread = [jnp.where(row == half * 64 + col // 2, 1.0, 0.0) for half in (0, 1)]
     gather = [jnp.where(col == half * 64 + row // 2, 1.0, 0.0) for half in (0, 1)]
-    return jnp.concatenate(spread, axis=1).astype(bf16), jnp.concatenate(gather, axis=0).astype(bf16)
+    quarter = [jnp.where(col == part * 32 + row // 4, 1.0, 0.0) for part in range(4)]
+    return jnp.concatenate(quarter, axis=0).astype(bf16), jnp.concatenate(spread, axis=1).astype(bf16), jnp.concatenate(gather, axis=0).astype(bf16)
 
 
 def dot(a, chosen):
@@ -37,7 +38,7 @@
     rhs_in, scale_in, mass_in, degrees, lower, upper, sol_out, res_out,
     rhs, scale, mass,
     gf, kf, cf, wf, df, sf, pf, jf, tmp_c, tmp_q, tmp_r,
-    gm, km, im, wm, dm, pm, jm, mid_c, mid_q, mid_r,
+    gm, km, im, wm, dm, pm, jm, mid_c, mid_q,
     lb, gl, kl, il, wl, dl, jl,
     coef, load_sem, send_sem, recv_sem, cycle_send, cycle_recv,
 ):
@@ -48,8 +49,6 @@
         pltpu.make_async_copy(src, dst, load_sem.at[i])
         for i, (src, dst) in enumerate(((scale_in, scale), (mass_in, mass), (rhs_in, rhs)))
     ]
-    for load in loads:
-        load.start()
 
     def clear(refs, first, planes, rows):
         for ref in refs:
@@ -86,7 +85,7 @@
         clear([ref.at[:, pl.ds(3, 2)] for ref in low_refs], 0, 13, (0, 4))
 
     barrier = pltpu.get_barrier_semaphore()
-    for step in range(1, 7):
+    for step in range(6, 0, -1):
         for sign in (1, -1):
             @pl.when((s + sign * step >= 0) & (s + sign * step < PEERS))
             def _(step=step, sign=sign):
@@ -96,6 +95,9 @@
             @pl.when((l + sign * step >= 0) & (l + sign * step < PEERS))
             def _(step=step, sign=sign):
                 pl.semaphore_signal(barrier, inc=1, device_id={"slab": s, "level": l + sign * step}, device_id_type=MESH)
+
+    for load in loads:
+        load.start()
 
     class Message:
         def __init__(self, src, dst, ds=0, dl=0, cycle=None):
@@ -177,7 +179,7 @@
             coef[grid, j, 1] = jnp.where(active, 2.0 * rho_new / radius, 0.0)
             rho = rho_new
 
-    spread, gather = split_matrices()
+    quarter, spread, gather = split_matrices()
     lane = lax.broadcasted_iota(jnp.int32, (1, LANES), 1)
 
     def tile_rows(v, rows):
@@ -268,11 +270,11 @@
             q = mass[z, :, cut]
             diag = c * c + q
             inverse = 1.0 / diag
-            tmp_c[z, t] = c
-            tmp_q[z, t] = q
+            tmp_c[z, t, pl.ds(0, 16), :] = c
+            tmp_q[z, t, pl.ds(0, 16), :] = q
             jf[z, t] = diag / c
             b = rhs[z, :, cut]
-            tmp_r[z, t] = b
+            tmp_r[z, t, pl.ds(0, 16), :] = b
             kf[6 + z, t, pl.ds(16, 16), :] = c * c * inverse * (1.0 / 26.0)
             cf[6 + z, t, pl.ds(16, 16), :] = c
             gf[0, 6 + z, t, pl.ds(16, 16), :] = c * inverse * b
@@ -308,9 +310,9 @@
         relay = x_messages(g, 2, 4, 16, cycle) + x_messages(g, 10, 4, 16, cycle)
         last = x_messages(g, 0, 2, 16, cycle) + x_messages(g, 14, 2, 16, cycle)
         low_z, mid_z = [], []
-        for hop in range(1, 7):
+        for hop in range(6, 0, -1):
             low_z += z_messages(low_view(cycle), 1, DEPTH, hop, cycle)
-        for hop in range(1, 4):
+        for hop in range(3, 0, -1):
             mid_z += z_messages(mid_view(gm.at[cycle]), 2, DEPTH, hop, cycle)
         low_x = low_x_messages(cycle, DEPTH, cycle)
         mid_x = x_messages(gm.at[cycle], 0, 14, 8, cycle)
@@ -322,24 +324,31 @@
                 for t in range(2):
                     c, q = cs[z][t], qs[z][t]
                     diag = c * c + q
-                    mid_c[z, t] = c
-                    mid_q[z, t] = q
+                    mid_c[z, t, pl.ds(0, 8), :] = c
+                    mid_q[z, t, pl.ds(0, 8), :] = q
                     jm[z, t] = c / diag
                     km[6 + z, t, pl.ds(16, 8), :] = c * c / diag * (1.0 / 26.0)
                     im[6 + z, t, pl.ds(16, 8), :] = 1.0 / c
             c, q = restrict(mid_c, 2, 2, 4)[0][0], restrict(mid_q, 2, 2, 4)[0][0]
             diag = c * c + q
-            jl[...] = c / diag
+            jl[pl.ds(0, 4), :] = c / diag
             lb[3, 6, 2] = c * c / diag * (1.0 / 26.0)
             lb[4, 6, 2] = 1.0 / c
 
+        sums = []
+        for t in range(4):
+            total = None
+            for z in range(4):
+                for dx in range(4):
+                    part = tmp_r[z, t, pl.ds(dx, 4, stride=4), :]
+                    total = part if total is None else total + part
+            sums.append(total * 0.25)
+        lb[cycle, 6, 2] = dot(jnp.concatenate(sums, axis=1), quarter) * jl[pl.ds(0, 4), :]
         rs = restrict(tmp_r, 4, 4, 8)
         for z in range(2):
             for t in range(2):
                 r = 4.0 * rs[z][t]
-                mid_r[z, t] = r
                 gm[cycle, 6 + z, t, pl.ds(16, 8), :] = r * jm[z, t]
-        lb[cycle, 6, 2] = 4.0 * restrict(mid_r, 2, 2, 4)[0][0] * jl[...]
 
         start(low_z)
 
@@ -428,7 +437,7 @@
         smooth(1, gm.at[cycle], km, wm, dm, 2, 2, [(8, 24)])
         cut = pl.ds(12, 16)
         coarse = jnp.concatenate([
-            wm[4, z, t, cut, :] * im[z, t, cut, :] + pm[(z - 6) // 2 + 1, t]
+            wm[4, z, t, cut, :] * im[z, t, cut, :] + pm[(z - 6) // 2 + 1, t, pl.ds(0, 16), :]
             for z in range(5, 9) for t in range(2)
         ], axis=0)
         wide = dot(coarse, spread)
@@ -438,8 +447,14 @@
                 for dx in (0, 1):
                     pf[z, t, pl.ds(dx, 16, stride=2), :] = wide[row:row + 16, half * LANES:(half + 1) * LANES]
 
+        opening(lambda: arrived(relay_k))
+        for z in range(5, 11):
+            for t in range(4):
+                cut = pl.ds(8, 32)
+                sf[z, t, cut, :] += 0.5 * (cf[z, t, cut, :] * pf[(z - 6) // 2 + 1, t, pl.ds(0, 32), :])
+
         arrived(side + relay)
-        opening(lambda: arrived(side_k + relay_k))
+        opening(lambda: arrived(side_k))
         chunks = [(8, 16), (24, 16)]
         smooth(0, g, kf, wf, df, 4, 4, chunks, lambda j: [(2 + j, 14 - j)])
 
@@ -450,8 +465,7 @@
         for z in range(5, 11):
             for t in range(4):
                 cut = pl.ds(8, 32)
-                step = 0.5 * (wf[4, z, t, cut, :] + cf[z, t, cut, :] * pf[(z - 6) // 2 + 1, t])
-                sf[z, t, cut, :] += step
+                sf[z, t, cut, :] += 0.5 * wf[4, z, t, cut, :]
 
         def residual(z, box):
             cut = pl.ds(16, 16)
@@ -460,10 +474,10 @@
                 scaled = gf[0, z, t, cut, :] - here + kf[z, t, cut, :] * (box[t] - here)
                 plain = scaled * jf[z - 6, t]
                 gf[cycle + 1, z, t, cut, :] = scaled
-                tmp_r[z - 6, t] = plain
+                tmp_r[z - 6, t, pl.ds(0, 16), :] = plain
                 out = pl.ds(t * LANES, LANES)
-                sol_out[z - 6, :, out] = here / cf[z, t, cut, :]
-                res_out[z - 6, :, out] = plain
+                sol_out[z - 6, :, out] = here
+                res_out[z - 6, :, out] = scaled
 
         sweep(sf, 6, 10, 4, 16, 16, residual)
         sent(every)
@@ -483,7 +497,7 @@
     block = jax.ShapeDtypeStruct(right_side.shape, f32)
     whole = pl.BlockSpec(memory_space=pltpu.VMEM)
     scalar = pl.BlockSpec(memory_space=pltpu.SMEM)
-    return pl.pallas_call(
+    weighted, scaled = pl.pallas_call(
         kernel,
         out_shape=(block, block),
         in_specs=[pl.BlockSpec(memory_space=pl.ANY)] * 3 + [scalar] * 3,
@@ -491,11 +505,11 @@
         scratch_shapes=[
             vmem(4, 16, 512), vmem(4, 16, 512), vmem(4, 16, 512),
             vmem(4, *fine), vmem(*fine), vmem(*fine), vmem(5, *fine), vmem(5, *fine), vmem(*fine),
-            vmem(4, 4, 32, LANES), vmem(4, 4, 16, LANES), vmem(4, 4, 16, LANES), vmem(4, 4, 16, LANES), vmem(4, 4, 16, LANES),
+            vmem(4, 4, 40, LANES), vmem(4, 4, 16, LANES), vmem(4, 4, 24, LANES), vmem(4, 4, 24, LANES), vmem(4, 4, 24, LANES),
             vmem(3, *mid), vmem(*mid), vmem(*mid), vmem(5, *mid), vmem(5, *mid),
-            vmem(3, 2, 16, LANES), vmem(2, 2, 8, LANES), vmem(2, 2, 8, LANES), vmem(2, 2, 8, LANES), vmem(2, 2, 8, LANES),
-            vmem(5, 13, 5, 4, LANES), vmem(*low), vmem(*low), vmem(*low), vmem(5, *low), vmem(5, *low),
-            vmem(4, LANES),
+            vmem(3, 2, 24, LANES), vmem(2, 2, 8, LANES), vmem(2, 2, 16, LANES), vmem(2, 2, 16, LANES),
+            vmem(6, 13, 5, 4, LANES), vmem(*low), vmem(*low), vmem(*low), vmem(5, *low), vmem(5, *low),
+            vmem(8, LANES),
             vmem(3, MAXDEG, 2, 8, LANES),
             pltpu.SemaphoreType.DMA((3,)),
             pltpu.SemaphoreType.DMA((ONCE,)), pltpu.SemaphoreType.DMA((ONCE,)),
@@ -505,6 +519,8 @@
             collective_id=0, has_side_effects=True, vmem_limit_bytes=56 * 1024 * 1024
         ),
     )(right_side, scale_field, mass_field, degrees, lower_bound, upper_bound)
+    inverse = 1.0 / scale_field
+    return weighted * inverse, scaled * (scale_field + mass_field * inverse)
 
 
 def solution(mesh):

time: 75.6 us -> 74.4 us (0.984)
  local copies, waits for them, and re-layouts: 2.26 us -> 0.01 us
  other arithmetic: 0 us -> 1.71 us
    unnamed x4, local copies, waits for them, and re-layouts: 2.26 us -> 0.01 us
    mul x0 -> x1, other arithmetic: none -> 1.71 us  [shards(): return (weighted * inverse, scaled * (scale_field + mass_field * inverse))]
where the time goes in v4:
time: 74.4 us; the launch traced here: 73.5 us
  Pallas kernels  71.1 us (96%)
  other arithmetic  1.71 us (2%)
    pallas_call x1, Pallas kernels, shards(): pl.pallas_call(kernel, out_shape=(block, block), in_specs=[pl.BlockSpec(m...  71.1 us
    mul x1, other arithmetic, shards(): return (weighted * inverse, scaled * (scale_field + mass_field * inverse))  1.71 us

profile of v4, /device:TPU:6, one launch (start us, length us, event | category | flops | bytes accessed | tf_op | source)
XLA Modules:
  0.0 73.5 jit_solution(17769633842886067004)
XLA Ops:
  0.6 0.0 copy-start.1
  0.6 0.0 copy-start
  0.7 71.1 %shard_map.77 = (f32[4,16,512]{2,1,0:T(8,128)}, f32[4,16,512]{2,1,0:T(8,128)}) custom-call(f32[4,16,512]{2,1,0:T(8,128)} %rhs_in.1, f32[4,16,512]{2,1,0:T(8,128)} %scale_in.1, f32[4,16,512]{2,1,0:T(8,128)} %mass_in.1, s32[3]{0:T(128)} %degrees.1, f32[3]{0:T(128)} %lower.1, f32[3]{0:T(128)} %upper.1), custom_call_target="tpu_custom_call" | custom-call | tf_op jit(solution)/shard_map/pallas_call | solution.py:500
  71.7 0.0 copy-done.1
  71.7 0.0 copy-done
  71.7 1.7 %add_multiply_fusion = (f32[4,16,512]{2,1,0:T(8,128)}, f32[4,16,512]{2,1,0:T(8,128)}) fusion(f32[4,16,512]{2,1,0:T(8,128)} %get-tuple-element.5, f32[4,16,512]{2,1,0:T(8,128)S(1)} %copy-done, f32[4,16,512]{2,1,0:T(8,128)S(1)} %copy-done.1, f32[4,16,512]{2,1,0:T(8,128)} %get-tuple-element.4), kind=kLoop, calls=%fused_computation | loop fusion | flops 163840 | bytes 786432 | tf_op jit(solution)/shard_map/mul | solution.py:523
Async XLA Ops:
  0.6 71.1 %copy-start.1 = (f32[4,16,512]{2,1,0:T(8,128)S(1)}, f32[4,16,512]{2,1,0:T(8,128)}, u32[]{:S(2)}) copy-start(f32[4,16,512]{2,1,0:T(8,128)} %mass_in.1) | copy-start | bytes 393220
  0.6 71.1 %copy-start = (f32[4,16,512]{2,1,0:T(8,128)S(1)}, f32[4,16,512]{2,1,0:T(8,128)}, u32[]{:S(2)}) copy-start(f32[4,16,512]{2,1,0:T(8,128)} %scale_in.1) | copy-start | bytes 393220

commit v5 on v4

--- a/solution.py
+++ b/solution.py
@@ -38,7 +38,7 @@
     rhs_in, scale_in, mass_in, degrees, lower, upper, sol_out, res_out,
     rhs, scale, mass,
     gf, kf, cf, wf, df, sf, pf, jf, tmp_c, tmp_q, tmp_r,
-    gm, km, im, wm, dm, pm, jm, mid_c, mid_q,
+    gm, km, im, wm, dm, pm, jm,
     lb, gl, kl, il, wl, dl, jl,
     coef, load_sem, send_sem, recv_sem, cycle_send, cycle_recv,
 ):
@@ -260,6 +260,17 @@
         return [
             [joined[rows * (z * half + o):rows * (z * half + o + 1)] for o in range(half)] for z in range(planes // 2)
         ]
+
+    def restrict_twice(src):
+        sums = []
+        for t in range(4):
+            total = None
+            for z in range(4):
+                for dx in range(4):
+                    part = src[z, t, pl.ds(dx, 4, stride=4), :]
+                    total = part if total is None else total + part
+            sums.append(total * (1.0 / 64.0))
+        return dot(jnp.concatenate(sums, axis=1), quarter)
 
     for load in loads:
         load.wait()
@@ -324,26 +335,16 @@
                 for t in range(2):
                     c, q = cs[z][t], qs[z][t]
                     diag = c * c + q
-                    mid_c[z, t, pl.ds(0, 8), :] = c
-                    mid_q[z, t, pl.ds(0, 8), :] = q
                     jm[z, t] = c / diag
                     km[6 + z, t, pl.ds(16, 8), :] = c * c / diag * (1.0 / 26.0)
                     im[6 + z, t, pl.ds(16, 8), :] = 1.0 / c
-            c, q = restrict(mid_c, 2, 2, 4)[0][0], restrict(mid_q, 2, 2, 4)[0][0]
+            c, q = restrict_twice(tmp_c), restrict_twice(tmp_q)
             diag = c * c + q
             jl[pl.ds(0, 4), :] = c / diag
             lb[3, 6, 2] = c * c / diag * (1.0 / 26.0)
             lb[4, 6, 2] = 1.0 / c
 
-        sums = []
-        for t in range(4):
-            total = None
-            for z in range(4):
-                for dx in range(4):
-                    part = tmp_r[z, t, pl.ds(dx, 4, stride=4), :]
-                    total = part if total is None else total + part
-            sums.append(total * 0.25)
-        lb[cycle, 6, 2] = dot(jnp.concatenate(sums, axis=1), quarter) * jl[pl.ds(0, 4), :]
+        lb[cycle, 6, 2] = 16.0 * restrict_twice(tmp_r) * jl[pl.ds(0, 4), :]
         rs = restrict(tmp_r, 4, 4, 8)
         for z in range(2):
             for t in range(2):
@@ -458,6 +459,8 @@
         chunks = [(8, 16), (24, 16)]
         smooth(0, g, kf, wf, df, 4, 4, chunks, lambda j: [(2 + j, 14 - j)])
 
+        sent(low_z + mid_z + near + side + far + relay + low_x + mid_x)
+        opening(lambda: sent(once))
         arrived(last)
         opening(lambda: arrived(last_k))
         smooth(0, g, kf, wf, df, 4, 4, chunks, lambda j: [(j, 2 + j), (14 - j, 16 - j)])
@@ -480,12 +483,11 @@
                 res_out[z - 6, :, out] = scaled
 
         sweep(sf, 6, 10, 4, 16, 16, residual)
-        sent(every)
+        sent(last)
         return carry
 
     lax.fori_loop(0, CYCLES, cycle_body, 0)
     assert len(once) <= ONCE and len(every) <= EVERY
-    sent(once)
 
 
 ONCE, EVERY = 80, 48
@@ -507,7 +509,7 @@
             vmem(4, *fine), vmem(*fine), vmem(*fine), vmem(5, *fine), vmem(5, *fine), vmem(*fine),
             vmem(4, 4, 40, LANES), vmem(4, 4, 16, LANES), vmem(4, 4, 24, LANES), vmem(4, 4, 24, LANES), vmem(4, 4, 24, LANES),
             vmem(3, *mid), vmem(*mid), vmem(*mid), vmem(5, *mid), vmem(5, *mid),
-            vmem(3, 2, 24, LANES), vmem(2, 2, 8, LANES), vmem(2, 2, 16, LANES), vmem(2, 2, 16, LANES),
+            vmem(3, 2, 24, LANES), vmem(2, 2, 8, LANES),
             vmem(6, 13, 5, 4, LANES), vmem(*low), vmem(*low), vmem(*low), vmem(5, *low), vmem(5, *low),
             vmem(8, LANES),
             vmem(3, MAXDEG, 2, 8, LANES),

time: 74.4 us -> 74.3 us (level)
  no operation moved by 1% of the time
where the time goes in v5:
time: 74.3 us; the launch traced here: 73.8 us
  Pallas kernels  71.5 us (96%)
  other arithmetic  1.71 us (2%)
    pallas_call x1, Pallas kernels, shards(): pl.pallas_call(kernel, out_shape=(block, block), in_specs=[pl.BlockSpec(m...  71.5 us
    mul x1, other arithmetic, shards(): return (weighted * inverse, scaled * (scale_field + mass_field * inverse))  1.71 us

profile of v5, /device:TPU:6, one launch (start us, length us, event | category | flops | bytes accessed | tf_op | source)
XLA Modules:
  0.0 73.8 jit_solution(1151108399057023913)
XLA Ops:
  0.6 0.0 copy-start.1
  0.6 0.0 copy-start
  0.7 71.5 %shard_map.77 = (f32[4,16,512]{2,1,0:T(8,128)}, f32[4,16,512]{2,1,0:T(8,128)}) custom-call(f32[4,16,512]{2,1,0:T(8,128)} %rhs_in.1, f32[4,16,512]{2,1,0:T(8,128)} %scale_in.1, f32[4,16,512]{2,1,0:T(8,128)} %mass_in.1, s32[3]{0:T(128)} %degrees.1, f32[3]{0:T(128)} %lower.1, f32[3]{0:T(128)} %upper.1), custom_call_target="tpu_custom_call" | custom-call | tf_op jit(solution)/shard_map/pallas_call | solution.py:502
  72.1 0.0 copy-done.1
  72.1 0.0 copy-done
  72.1 1.7 %add_multiply_fusion = (f32[4,16,512]{2,1,0:T(8,128)}, f32[4,16,512]{2,1,0:T(8,128)}) fusion(f32[4,16,512]{2,1,0:T(8,128)} %get-tuple-element.5, f32[4,16,512]{2,1,0:T(8,128)S(1)} %copy-done, f32[4,16,512]{2,1,0:T(8,128)S(1)} %copy-done.1, f32[4,16,512]{2,1,0:T(8,128)} %get-tuple-element.4), kind=kLoop, calls=%fused_computation | loop fusion | flops 163840 | bytes 786432 | tf_op jit(solution)/shard_map/mul | solution.py:525
Async XLA Ops:
  0.6 71.5 %copy-start.1 = (f32[4,16,512]{2,1,0:T(8,128)S(1)}, f32[4,16,512]{2,1,0:T(8,128)}, u32[]{:S(2)}) copy-start(f32[4,16,512]{2,1,0:T(8,128)} %mass_in.1) | copy-start | bytes 393220
  0.6 71.5 %copy-start = (f32[4,16,512]{2,1,0:T(8,128)S(1)}, f32[4,16,512]{2,1,0:T(8,128)}, u32[]{:S(2)}) copy-start(f32[4,16,512]{2,1,0:T(8,128)} %scale_in.1) | copy-start | bytes 393220
